TPU v7x, 128 devices: a whole 4x4x4 slice. The times are simulated.
128 devices in a mesh: lat: 8 (over x, core), lon: 16 (over y, z).
Axes of the slice: x: 4, y: 4, z: 4, core: 2. Of those that a mesh axis runs over, the one named last changes fastest.
Arguments:
- node_latent: bfloat16 [32768, 512], P(('lat', 'lon')), may hold values from -6 to 6
- edge_latent: bfloat16 [262144, 512], P(('lat', 'lon')), may hold values from -6 to 6
- sender_slot: int32 [262144], P(('lat', 'lon')), may hold values from 0 to 1279, as said below
- receiver: int32 [262144], P(('lat', 'lon')), may hold values from 0 to 255
- border_list: int32 [128, 2, 2, 32], P(('lat', 'lon')), may hold values from 0 to 255
- send_list: int32 [128, 128, 4], P(('lat', 'lon')), may hold values from 0 to 255
- edge_count: int32 [128], P(('lat', 'lon')), may hold values from 1024 to 2048, as said below
- edge_weight: bfloat16 [512, 512], replicated, may hold values from -0.25 to 0.25
- sender_weight: bfloat16 [512, 512], replicated, may hold values from -0.25 to 0.25
- receiver_weight: bfloat16 [512, 512], replicated, may hold values from -0.25 to 0.25
- hidden_bias: float32 [512], replicated, may hold values from -3 to 3
- message_weight: bfloat16 [512, 512], replicated, may hold values from -0.25 to 0.25
- message_bias: float32 [512], replicated, may hold values from -3 to 3
- edge_scales: float32 [512], replicated, may hold values from 0.25 to 1.75
- self_weight: bfloat16 [512, 512], replicated, may hold values from -0.25 to 0.25
- summed_weight: bfloat16 [512, 512], replicated, may hold values from -0.25 to 0.25
- node_bias: float32 [512], replicated, may hold values from -3 to 3
- update_weight: bfloat16 [512, 512], replicated, may hold values from -0.25 to 0.25
- update_bias: float32 [512], replicated, may hold values from -3 to 3
- node_scales: float32 [512], replicated, may hold values from 0.25 to 1.75
- node_cotangent: bfloat16 [32768, 512], P(('lat', 'lon')), may hold values from -6 to 6
- edge_cotangent: bfloat16 [262144, 512], P(('lat', 'lon')), may hold values from -6 to 6
Outputs:
- node_result: bfloat16 [32768, 512], P(('lat', 'lon'))
- edge_result: bfloat16 [262144, 512], P(('lat', 'lon'))
- node_grad: float32 [32768, 512], P(('lat', 'lon'))
- edge_grad: float32 [262144, 512], P(('lat', 'lon'))
Inputs may be any that keep to these rules, and one draw needn't show every extreme that they name: `sender_slot`: most edges take a sender from their own partition's rows, most others from the border block; border cells beyond the latitude ends are never named. `border_list`: rows of one border group may repeat. `send_list`: rows of one send list may repeat. `edge_count`: some partition has all 2048 slots live.
All inputs are finite; a program needn't handle non-finite values.
Results may differ from a plain program's by a relative error of at most 0.015.
Values may be sent and summed in bfloat16 or wider, within the bound.
A program may use at most 128 MiB of HBM per device.

v0:
```python
import jax
import jax.numpy as jnp
from jax import lax
from jax.sharding import PartitionSpec as P


def padded(value, sides, width, wrap):
    for axis, dim in sides:
        devices, length = (lax.axis_size(axis), value.shape[dim])
        up = [(i, (i + 1) % devices) for i in range(devices if wrap else devices - 1)]
        down = [(j, i) for i, j in up]
        last = lax.slice_in_dim(value, length - width, length, axis=dim)
        initial = lax.slice_in_dim(value, 0, width, axis=dim)
        before = lax.ppermute(last, axis, up)
        after = lax.ppermute(initial, axis, down)
        value = jnp.concatenate([before, value, after], axis=dim)
    return value


def layer_norm(values, scales):
    average = jnp.mean(values, -1, keepdims=True)
    centred = values - average
    scatter_result = jnp.mean(centred * centred, -1, keepdims=True)
    return centred * lax.rsqrt(scatter_result + 1e-05) * scales


def local_layer(node_wide, table, edge_widened, sender_slot, receiver, active_count, weights):
    (
        edge_weight,
        sender_weight,
        receiver_weight,
        hidden_bias,
        message_weight,
        message_bias,
        edge_scales,
        self_weight,
        summed_weight,
        node_bias,
        update_weight,
        update_bias,
        node_scales,
    ) = weights
    sender_rows = table[sender_slot]
    receiver_rows = node_wide[receiver]
    hidden = (
        jnp.dot(edge_widened.astype(jnp.bfloat16), edge_weight, preferred_element_type=jnp.float32)
        + jnp.dot(
            sender_rows.astype(jnp.bfloat16), sender_weight, preferred_element_type=jnp.float32
        )
        + jnp.dot(
            receiver_rows.astype(jnp.bfloat16), receiver_weight, preferred_element_type=jnp.float32
        )
        + hidden_bias
    )
    hidden = jax.nn.silu(hidden).astype(jnp.bfloat16)
    edge_message = layer_norm(
        jnp.dot(hidden, message_weight, preferred_element_type=jnp.float32) + message_bias,
        edge_scales,
    )
    active_mask = (jnp.arange(edge_widened.shape[0], dtype=jnp.int32) < active_count).astype(
        jnp.float32
    )
    edge_message = edge_message * active_mask[:, None]
    edge_result = (edge_widened + edge_message).astype(jnp.bfloat16)
    one_hot = (
        receiver[None, :] == jnp.arange(node_wide.shape[0], dtype=jnp.int32)[:, None]
    ).astype(jnp.bfloat16)
    summed = jnp.dot(
        one_hot, edge_message.astype(jnp.bfloat16), preferred_element_type=jnp.float32
    ).astype(jnp.bfloat16)
    inner = (
        jnp.dot(node_wide.astype(jnp.bfloat16), self_weight, preferred_element_type=jnp.float32)
        + jnp.dot(summed, summed_weight, preferred_element_type=jnp.float32)
        + node_bias
    )
    inner = jax.nn.silu(inner).astype(jnp.bfloat16)
    update = layer_norm(
        jnp.dot(inner, update_weight, preferred_element_type=jnp.float32) + update_bias, node_scales
    )
    node_result = (node_wide + update).astype(jnp.bfloat16)
    return (node_result, edge_result)


def per_device(
    node_latent,
    edge_latent,
    sender_slot,
    receiver,
    border_list,
    send_list,
    edge_count,
    edge_weight,
    sender_weight,
    receiver_weight,
    hidden_bias,
    message_weight,
    message_bias,
    edge_scales,
    self_weight,
    summed_weight,
    node_bias,
    update_weight,
    update_bias,
    node_scales,
    node_cotangent,
    edge_cotangent,
):
    weights = (
        edge_weight,
        sender_weight,
        receiver_weight,
        hidden_bias,
        message_weight,
        message_bias,
        edge_scales,
        self_weight,
        summed_weight,
        node_bias,
        update_weight,
        update_bias,
        node_scales,
    )
    width = node_latent.shape[1]
    lat_size = lax.axis_size("lat")
    lon_size = lax.axis_size("lon")
    groups = border_list[0]
    boundary_rows = groups.shape[2]
    own_groups = node_latent[groups]
    banded = padded(own_groups, (("lat", 0),), 1, False)
    cycle = padded(banded, (("lon", 1),), 1, True)
    cycle_wide = cycle.reshape(-1, width).astype(jnp.float32)
    row_lists = send_list[0]
    slots = row_lists.shape[1]
    outgoing = node_latent[row_lists]
    arriving = lax.all_to_all(outgoing, ("lat", "lon"), split_axis=0, concat_axis=0, tiled=True)
    received = arriving.reshape(-1, width).astype(jnp.float32)
    active_count = edge_count[0]

    def local_part(node_wide, border_wide, far_wide, edge_widened):
        table = jnp.concatenate([node_wide, border_wide, far_wide], 0)
        return local_layer(
            node_wide, table, edge_widened, sender_slot, receiver, active_count, weights
        )

    results, pull = jax.vjp(
        local_part,
        node_latent.astype(jnp.float32),
        cycle_wide,
        received,
        edge_latent.astype(jnp.float32),
    )
    node_grad, border_grad, slot_grad, edge_grad = pull((node_cotangent, edge_cotangent))
    border_grad = border_grad.reshape(4, 4, boundary_rows, width)
    widened = padded(border_grad.astype(jnp.bfloat16), (("lon", 1),), 1, True).astype(
        border_grad.dtype
    )
    padded_latents = padded(widened.astype(jnp.bfloat16), (("lat", 0),), 1, False).astype(
        widened.dtype
    )
    folded = padded_latents.reshape(2, 3, 2, 3, boundary_rows, width)[:, ::2][:, :, :, ::2].sum(
        (1, 3)
    )
    node_grad = node_grad.at[groups.reshape(-1)].add(folded.reshape(-1, width))
    returned = lax.all_to_all(
        slot_grad.reshape(lat_size * lon_size, slots, width).astype(jnp.bfloat16),
        ("lat", "lon"),
        split_axis=0,
        concat_axis=0,
        tiled=True,
    ).astype(jnp.float32)
    node_grad = node_grad.at[row_lists.reshape(-1)].add(returned.reshape(-1, width))
    return (results[0], results[1], node_grad, edge_grad)


def solution(mesh):
    placed = (
        P(("lat", "lon"), None),
        P(("lat", "lon"), None),
        P(("lat", "lon")),
        P(("lat", "lon")),
        P(("lat", "lon"), None, None, None),
        P(("lat", "lon"), None, None),
        P(("lat", "lon")),
        P(),
        P(),
        P(),
        P(),
        P(),
        P(),
        P(),
        P(),
        P(),
        P(),
        P(),
        P(),
        P(),
        P(("lat", "lon"), None),
        P(("lat", "lon"), None),
    )
    return jax.shard_map(
        per_device,
        mesh=mesh,
        in_specs=placed,
        out_specs=(
            P(("lat", "lon"), None),
            P(("lat", "lon"), None),
            P(("lat", "lon"), None),
            P(("lat", "lon"), None),
        ),
        check_vma=False,
    )
```

profile of v0, /device:TPU:1, one launch (start us, length us, event | category | flops | bytes accessed | tf_op | source)
XLA Modules:
  0.0 184.5 jit_solution(13403112489656915822)
XLA Ops:
  1.7 3.8 %gather_fusion.1 = bf16[512,512]{1,0:T(8,128)(2,1)} fusion(bf16[256,512]{1,0:T(8,128)(2,1)} %param.22, s32[1024]{0:T(1024)S(1)} %pad_clamp_fusion), kind=kCustom, calls=%fused_computation.1 | custom fusion | bytes 1050624 | tf_op jit(solution)/shard_map/gather | solution.py:134
  7.5 12.0 %all-to-all-start = ((bf16[128,4,512]{2,1,0:T(4,128)(2,1)}), bf16[128,4,512]{2,1,0:T(4,128)(2,1)}, u32[]{:S(2)}, u32[]{:S(2)}) async-start(bf16[128,4,512]{2,1,0:T(4,128)(2,1)} %reshape.219), calls=%async_computation | async-start | bytes 1048576 | tf_op jit(solution)/shard_map/all_to_all | solution.py:135
  21.0 3.0 %collective-permute-start.1 = (bf16[1,2,32,512]{3,2,1,0:T(8,128)(2,1)}, bf16[1,2,32,512]{3,2,1,0:T(8,128)(2,1)}, u32[]{:S(2)}, u32[]{:S(2)}) collective-permute-start(bf16[1,2,32,512]{3,2,1,0:T(8,128)(2,1)} %bitcast.3), channel_id=1, source_target_pairs={{16,0},{32,16},{48,32},{64,48},{80,64},{96,80},{112,96},{17,1},{33... | collective-permute-start | bytes 196616 | tf_op jit(solution)/shard_map/ppermute | solution.py:15
  24.1 2.5 %collective-permute-start = (bf16[1,2,32,512]{3,2,1,0:T(8,128)(2,1)}, bf16[1,2,32,512]{3,2,1,0:T(8,128)(2,1)}, u32[]{:S(2)}, u32[]{:S(2)}) collective-permute-start(bf16[1,2,32,512]{3,2,1,0:T(8,128)(2,1)} %bitcast.1), channel_id=1, source_target_pairs={{0,16},{16,32},{32,48},{48,64},{64,80},{80,96},{96,112},{1,17},{17... | collective-permute-start | bytes 196616 | tf_op jit(solution)/shard_map/ppermute | solution.py:14
  32.9 3.3 %fusion.59 = f32[2048,512]{1,0:T(8,128)} fusion(bf16[2048,512]{1,0:T(8,128)(2,1)S(1)} %copy-done.8, bf16[512,512]{1,0:T(8,128)(2,1)S(1)} %copy-done.16), kind=kOutput, calls=%fused_computation.117 | convolution fusion | flops 1073741824 | bytes 6815744 | tf_op jit(solution)/shard_map/jvp()/dot_general | solution.py:46
  39.1 5.6 %collective-permute-start.3 = (bf16[4,1,32,512]{3,2,1,0:T(8,128)(2,1)S(1)}, bf16[4,1,32,512]{3,2,1,0:T(8,128)(2,1)S(1)}, u32[]{:S(2)}, u32[]{:S(2)}) collective-permute-start(bf16[4,1,32,512]{3,2,1,0:T(8,128)(2,1)S(1)} %get-tuple-element.26), channel_id=1, source_target_pairs={{1,0},{2,1},{3,2},{4,3},{5,4},{6,5},{7,6},{8,7},{9,8},{10,9},{11,1... | collective-permute-start | bytes 393224 | tf_op jit(solution)/shard_map/ppermute | solution.py:15
  48.3 9.2 %gather_fusion.3 = bf16[2048,512]{1,0:T(8,128)(2,1)} fusion(bf16[256,512]{1,0:T(8,128)(2,1)S(1)} %copy-done.2, s32[2048]{0:T(1024)S(1)} %get-tuple-element.30), kind=kCustom, calls=%fused_computation.3 | custom fusion | bytes 4202496 | tf_op jit(solution)/shard_map/jvp()/gather | solution.py:44
  63.0 9.2 %gather_fusion.2 = bf16[2048,512]{1,0:T(8,128)(2,1)} fusion(bf16[1280,512]{1,0:T(8,128)(2,1)S(1)} %pad_maximum_fusion, s32[2048]{0:T(1024)S(1)} %get-tuple-element.32), kind=kCustom, calls=%fused_computation.2 | custom fusion | bytes 4202496 | tf_op jit(solution)/shard_map/jvp()/gather | solution.py:43
  72.2 3.0 %fusion.62 = f32[2048,512]{1,0:T(8,128)S(1)} fusion(bf16[2048,512]{1,0:T(8,128)(2,1)} %gather_fusion.2, bf16[512,512]{1,0:T(8,128)(2,1)S(1)} %copy-done.21), kind=kOutput, calls=%fused_computation.120 | convolution fusion | flops 1073741824 | bytes 6815744 | tf_op jit(solution)/shard_map/jvp()/dot_general | solution.py:47
  81.8 4.5 %fusion.24 = f32[256,512]{1,0:T(8,128)} fusion(f32[256,512]{1,0:T(8,128)S(1)} %copy-done.25, bf16[512,512]{1,0:T(8,128)(2,1)S(1)} %copy-done.39, f32[2048,512]{0,1:T(8,128)} %copy-done.6, f32[2048]{0:T(1024)S(1)} %fusion.45, f32[512]{0:T(512)S(1)} %copy-done.36, f32[2048]{0:T(1024)S(1)} %fusion.46, f32[2048]{0:T(1024)S(1)} %broadcast_multiply_fusion, ...), kind=kOutput, calls=%fused_computation.50 | convolution fusion | flops 678297600 | bytes 5806080 | tf_op jit(solution)/shard_map/jvp()/dot_general | solution.py:73
  89.9 5.7 %multiply_reduce_fusion = (f32[2048]{0:T(1024)S(1)}, bf16[2048,512]{0,1:T(8,128)(2,1)}) fusion(bf16[2048,512]{0,1:T(8,128)(2,1)S(1)} %copy-done.4, f32[2048,512]{0,1:T(8,128)} %copy-done.6, f32[2048]{0:T(1024)S(1)} %fusion.45, f32[512]{0:T(512)S(1)} %copy-done.36, f32[2048]{0:T(1024)S(1)} %broadcast_multiply_fusion, f32[512]{0:T(512)S(1)} %copy-done.28, ...), kind=kOutput, calls=%fused_computation.24 | convolution fusion | flops 682096640 | bytes 9211904 | tf_op jit(solution)/shard_map/transpose(jvp())/dot_general | solution.py:68
  95.6 6.3 %fusion.52 = (f32[2048]{0:T(1024)S(1)}, f32[2048,512]{0,1:T(8,128)S(1)}, bf16[2048,512]{0,1:T(8,128)(2,1)}) fusion(f32[2048]{0:T(1024)S(1)} %multiply_multiply_fusion.1, f32[2048]{0:T(1024)S(1)} %broadcast_multiply_fusion, f32[2048,512]{0,1:T(8,128)} %copy-done.6, f32[512]{0:T(512)S(1)} %copy-done.28, f32[2048]{0:T(1024)S(1)} %fusion.46, ...), kind=kLoop, calls=%fused_computation.110 | loop fusion | flops 18872320 | bytes 16822272 | tf_op jit(solution)/shard_map/transpose(jvp())/reduce_sum | solution.py:22
  101.9 2.6 %fusion.2 = bf16[2048,512]{1,0:T(8,128)(2,1)S(1)} fusion(f32[2048,512]{1,0:T(8,128)S(1)} %copy-done.13, bf16[512,512]{1,0:T(8,128)(2,1)S(1)} %copy-done, f32[2048,512]{0,1:T(8,128)S(1)} %get-tuple-element.15, f32[2048]{0:T(1024)S(1)} %negate_multiply_fusion), kind=kOutput, calls=%fused_computation.16 | convolution fusion | flops 1087373312 | bytes 11018240 | tf_op jit(solution)/shard_map/transpose(jvp())/dot_general | solution.py:57
  104.6 2.6 %fusion.61 = bf16[2048,512]{1,0:T(8,128)(2,1)} fusion(bf16[2048,512]{1,0:T(8,128)(2,1)S(1)} %fusion.2, bf16[512,512]{1,0:T(8,128)(2,1)S(1)} %copy-done.22), kind=kOutput, calls=%fused_computation.119 | convolution fusion | flops 1073741824 | bytes 4718592 | tf_op jit(solution)/shard_map/transpose(jvp())/dot_general | solution.py:47
  107.2 3.2 %convert_add_fusion = f32[2048,512]{0,1:T(8,128)} fusion(bf16[2048,512]{0,1:T(8,128)(2,1)S(1)} %copy-done.4, bf16[2048,512]{1,0:T(8,128)(2,1)S(1)} %fusion.2, bf16[512,512]{1,0:T(8,128)(2,1)S(1)} %copy-done.17), kind=kOutput, calls=%fused_computation.12 | convolution fusion | flops 1076887552 | bytes 8912896 | tf_op jit(solution)/shard_map/transpose(jvp())/dot_general | solution.py:46
  110.4 14.0 %scatter_custom_fusion = f32[1280,512]{1,0:T(8,128)S(1)} fusion(s32[2048]{0:T(1024)} %get-tuple-element.31, bf16[2048,512]{1,0:T(8,128)(2,1)} %fusion.61, f32[]{:T(128)} %constant.14.clone.1), kind=kCustom, calls=%fused_computation.20 | custom fusion | flops 2097152 | bytes 4719104 | tf_op jit(solution)/shard_map/transpose(jvp())/scatter-add | solution.py:43
  126.2 4.8 %collective-permute-start.5 = (bf16[4,1,32,512]{3,2,1,0:T(8,128)(2,1)}, bf16[4,1,32,512]{3,2,1,0:T(8,128)(2,1)S(1)}, u32[]{:S(2)}, u32[]{:S(2)}) collective-permute-start(bf16[4,1,32,512]{3,2,1,0:T(8,128)(2,1)} %get-tuple-element.24), channel_id=1, source_target_pairs={{1,0},{2,1},{3,2},{4,3},{5,4},{6,5},{7,6},{8,7},{9,8},{10,9},{11,1... | collective-permute-start | bytes 393224 | tf_op jit(solution)/shard_map/ppermute | solution.py:15
  130.9 2.7 %fusion.60 = bf16[2048,512]{1,0:T(8,128)(2,1)} fusion(bf16[2048,512]{1,0:T(8,128)(2,1)S(1)} %copy-done.11, bf16[512,512]{1,0:T(8,128)(2,1)S(1)} %copy-done.24), kind=kOutput, calls=%fused_computation.118 | convolution fusion | flops 1073741824 | bytes 4718592 | tf_op jit(solution)/shard_map/transpose(jvp())/dot_general | solution.py:50
  133.6 4.0 %copy.36 = bf16[2048,512]{1,0:T(8,128)(2,1)} copy(bf16[2048,512]{0,1:T(8,128)(2,1)} %get-tuple-element.16) | data formatting | bytes 4194304
  138.5 9.4 %all-to-all-start.1 = ((bf16[128,4,512]{2,1,0:T(4,128)(2,1)}), bf16[128,4,512]{2,1,0:T(4,128)(2,1)}, u32[]{:S(2)}, u32[]{:S(2)}) async-start(bf16[128,4,512]{2,1,0:T(4,128)(2,1)} %convert_element_type.152), calls=%async_computation.1 | async-start | bytes 1048576 | tf_op jit(solution)/shard_map/all_to_all | solution.py:164
  148.0 5.5 %copy.37 = f32[2048,512]{1,0:T(8,128)} copy(f32[2048,512]{0,1:T(8,128)} %convert_add_fusion) | data formatting | bytes 8388608
  155.0 3.0 %collective-permute-start.7 = (bf16[1,6,32,512]{3,2,1,0:T(8,128)(2,1)}, bf16[1,6,32,512]{3,2,1,0:T(8,128)(2,1)}, u32[]{:S(2)}, u32[]{:S(2)}) collective-permute-start(bf16[1,6,32,512]{3,2,1,0:T(8,128)(2,1)} %get-tuple-element.20), channel_id=1, source_target_pairs={{16,0},{32,16},{48,32},{64,48},{80,64},{96,80},{112,96},{17,1},{33... | collective-permute-start | bytes 589832 | tf_op jit(solution)/shard_map/ppermute | solution.py:15
  162.3 13.4 %scatter_custom_fusion.1 = f32[256,512]{1,0:T(8,128)S(1)} fusion(f32[256,512]{1,0:T(8,128)S(1)} %fusion.30, s32[2048]{0:T(1024)} %get-tuple-element.29, bf16[2048,512]{1,0:T(8,128)(2,1)S(1)} %copy-done.18), kind=kCustom, calls=%fused_computation.18 | custom fusion | flops 2097152 | bytes 2621440 | tf_op jit(solution)/shard_map/transpose(jvp())/scatter-add | solution.py:44
  179.9 3.8 %scatter_fusion.1 = f32[256,512]{1,0:T(8,128)S(1)} fusion(f32[256,512]{1,0:T(8,128)S(1)} %scatter_fusion, s32[512]{0:T(512)S(1)} %bitcast.54, f32[512,512]{1,0:T(8,128)S(1)} %reshape.270), kind=kCustom, calls=%fused_computation.7 | custom fusion | flops 262144 | bytes 3147776 | tf_op jit(solution)/shard_map/scatter-add | solution.py:171
  (150 shorter events, 45.4 us)
Async XLA Ops:
  0.6 76.4 %copy-start = (bf16[512,512]{1,0:T(8,128)(2,1)S(1)}, bf16[512,512]{1,0:T(8,128)(2,1)}, u32[]{:S(2)}) copy-start(bf16[512,512]{1,0:T(8,128)(2,1)} %param.33) | copy-start | bytes 1572868
  0.6 18.9 %copy-start.2 = (bf16[256,512]{1,0:T(8,128)(2,1)S(1)}, bf16[256,512]{1,0:T(8,128)(2,1)}, u32[]{:S(2)}) copy-start(bf16[256,512]{1,0:T(8,128)(2,1)} %param.22) | copy-start | bytes 786436
  0.7 18.8 %copy-start.34 = (s32[1,2,2,32]{3,2,1,0:T(2,128)S(1)}, s32[1,2,2,32]{3,2,1,0:T(2,128)}, u32[]{:S(2)}) copy-start(s32[1,2,2,32]{3,2,1,0:T(2,128)} %param.26) | copy-start | bytes 1540
  1.5 25.1 %copy-start.32 = (s32[1,128,4]{1,2,0:T(4,128)S(1)}, s32[1,128,4]{1,2,0:T(4,128)}, u32[]{:S(2)}) copy-start(s32[1,128,4]{1,2,0:T(4,128)} %param.27) | copy-start | bytes 6148
  1.7 27.8 %copy-start.30 = (s32[2048]{0:T(1024)S(1)}, s32[2048]{0:T(1024)}, u32[]{:S(2)}) copy-start(s32[2048]{0:T(1024)} %param.24) | copy-start | bytes 24580
  1.7 31.2 %copy-start.8 = (bf16[2048,512]{1,0:T(8,128)(2,1)S(1)}, bf16[2048,512]{1,0:T(8,128)(2,1)}, u32[]{:S(2)}) copy-start(bf16[2048,512]{1,0:T(8,128)(2,1)} %param.23) | copy-start | bytes 6291460
  1.7 31.2 %copy-start.16 = (bf16[512,512]{1,0:T(8,128)(2,1)S(1)}, bf16[512,512]{1,0:T(8,128)(2,1)}, u32[]{:S(2)}) copy-start(bf16[512,512]{1,0:T(8,128)(2,1)} %param.29) | copy-start | bytes 1572868
  7.5 54.2 %all-to-all-start = ((bf16[128,4,512]{2,1,0:T(4,128)(2,1)}), bf16[128,4,512]{2,1,0:T(4,128)(2,1)}, u32[]{:S(2)}, u32[]{:S(2)}) async-start(bf16[128,4,512]{2,1,0:T(4,128)(2,1)} %reshape.219), calls=%async_computation | async-start | bytes 1048576 | tf_op jit(solution)/shard_map/all_to_all | solution.py:135
  21.0 17.1 %collective-permute-start.1 = (bf16[1,2,32,512]{3,2,1,0:T(8,128)(2,1)}, bf16[1,2,32,512]{3,2,1,0:T(8,128)(2,1)}, u32[]{:S(2)}, u32[]{:S(2)}) collective-permute-start(bf16[1,2,32,512]{3,2,1,0:T(8,128)(2,1)} %bitcast.3), channel_id=1, source_target_pairs={{16,0},{32,16},{48,32},{64,48},{80,64},{96,80},{112,96},{17,1},{33... | collective-permute-start | bytes 196616 | tf_op jit(solution)/shard_map/ppermute | solution.py:15
  24.1 14.0 %collective-permute-start = (bf16[1,2,32,512]{3,2,1,0:T(8,128)(2,1)}, bf16[1,2,32,512]{3,2,1,0:T(8,128)(2,1)}, u32[]{:S(2)}, u32[]{:S(2)}) collective-permute-start(bf16[1,2,32,512]{3,2,1,0:T(8,128)(2,1)} %bitcast.1), channel_id=1, source_target_pairs={{0,16},{16,32},{32,48},{48,64},{64,80},{80,96},{96,112},{1,17},{17... | collective-permute-start | bytes 196616 | tf_op jit(solution)/shard_map/ppermute | solution.py:14
  39.1 21.6 %collective-permute-start.3 = (bf16[4,1,32,512]{3,2,1,0:T(8,128)(2,1)S(1)}, bf16[4,1,32,512]{3,2,1,0:T(8,128)(2,1)S(1)}, u32[]{:S(2)}, u32[]{:S(2)}) collective-permute-start(bf16[4,1,32,512]{3,2,1,0:T(8,128)(2,1)S(1)} %get-tuple-element.26), channel_id=1, source_target_pairs={{1,0},{2,1},{3,2},{4,3},{5,4},{6,5},{7,6},{8,7},{9,8},{10,9},{11,1... | collective-permute-start | bytes 393224 | tf_op jit(solution)/shard_map/ppermute | solution.py:15
  44.7 16.0 %collective-permute-start.2 = (bf16[4,1,32,512]{3,2,1,0:T(8,128)(2,1)S(1)}, bf16[4,1,32,512]{3,2,1,0:T(8,128)(2,1)S(1)}, u32[]{:S(2)}, u32[]{:S(2)}) collective-permute-start(bf16[4,1,32,512]{3,2,1,0:T(8,128)(2,1)S(1)} %get-tuple-element.25), channel_id=1, source_target_pairs={{0,1},{1,2},{2,3},{3,4},{4,5},{5,6},{6,7},{7,8},{8,9},{9,10},{10,1... | collective-permute-start | bytes 393224 | tf_op jit(solution)/shard_map/ppermute | solution.py:14
  48.3 9.9 %copy-start.19 = (bf16[2048,512]{1,0:T(8,128)(2,1)S(1)}, bf16[2048,512]{1,0:T(8,128)(2,1)}, u32[]{:S(2)}) copy-start(bf16[2048,512]{1,0:T(8,128)(2,1)} %param.43) | copy-start | bytes 6291460
  62.9 9.2 %copy-start.21 = (bf16[512,512]{1,0:T(8,128)(2,1)S(1)}, bf16[512,512]{1,0:T(8,128)(2,1)}, u32[]{:S(2)}) copy-start(bf16[512,512]{1,0:T(8,128)(2,1)} %param.30) | copy-start | bytes 1572868
  124.4 9.3 %copy-start.7 = (f32[1280,512]{1,0:T(8,128)}, f32[1280,512]{1,0:T(8,128)S(1)}, u32[]{:S(2)}) copy-start(f32[1280,512]{1,0:T(8,128)S(1)} %scatter_custom_fusion) | copy-start | bytes 7864324
  124.4 6.6 %copy-start.11 = (bf16[2048,512]{1,0:T(8,128)(2,1)S(1)}, bf16[2048,512]{1,0:T(8,128)(2,1)}, u32[]{:S(2)}) copy-start(bf16[2048,512]{1,0:T(8,128)(2,1)} %copy-done.10) | copy-start | bytes 6291460
  126.2 27.3 %collective-permute-start.5 = (bf16[4,1,32,512]{3,2,1,0:T(8,128)(2,1)}, bf16[4,1,32,512]{3,2,1,0:T(8,128)(2,1)S(1)}, u32[]{:S(2)}, u32[]{:S(2)}) collective-permute-start(bf16[4,1,32,512]{3,2,1,0:T(8,128)(2,1)} %get-tuple-element.24), channel_id=1, source_target_pairs={{1,0},{2,1},{3,2},{4,3},{5,4},{6,5},{7,6},{8,7},{9,8},{10,9},{11,1... | collective-permute-start | bytes 393224 | tf_op jit(solution)/shard_map/ppermute | solution.py:15
  130.9 22.5 %collective-permute-start.4 = (bf16[4,1,32,512]{3,2,1,0:T(8,128)(2,1)}, bf16[4,1,32,512]{3,2,1,0:T(8,128)(2,1)}, u32[]{:S(2)}, u32[]{:S(2)}) collective-permute-start(bf16[4,1,32,512]{3,2,1,0:T(8,128)(2,1)} %get-tuple-element.23), channel_id=1, source_target_pairs={{0,1},{1,2},{2,3},{3,4},{4,5},{5,6},{6,7},{7,8},{8,9},{9,10},{10,1... | collective-permute-start | bytes 393224 | tf_op jit(solution)/shard_map/ppermute | solution.py:14
  138.5 40.2 %all-to-all-start.1 = ((bf16[128,4,512]{2,1,0:T(4,128)(2,1)}), bf16[128,4,512]{2,1,0:T(4,128)(2,1)}, u32[]{:S(2)}, u32[]{:S(2)}) async-start(bf16[128,4,512]{2,1,0:T(4,128)(2,1)} %convert_element_type.152), calls=%async_computation.1 | async-start | bytes 1048576 | tf_op jit(solution)/shard_map/all_to_all | solution.py:164
  147.9 12.7 %copy-start.15 = (bf16[256,512]{1,0:T(8,128)(2,1)S(1)}, bf16[256,512]{1,0:T(8,128)(2,1)}, u32[]{:S(2)}) copy-start(bf16[256,512]{1,0:T(8,128)(2,1)} %param.42) | copy-start | bytes 786436
  147.9 14.3 %copy-start.18 = (bf16[2048,512]{1,0:T(8,128)(2,1)S(1)}, bf16[2048,512]{1,0:T(8,128)(2,1)}, u32[]{:S(2)}) copy-start(bf16[2048,512]{1,0:T(8,128)(2,1)} %fusion.60) | copy-start | bytes 6291460
  155.0 20.7 %collective-permute-start.7 = (bf16[1,6,32,512]{3,2,1,0:T(8,128)(2,1)}, bf16[1,6,32,512]{3,2,1,0:T(8,128)(2,1)}, u32[]{:S(2)}, u32[]{:S(2)}) collective-permute-start(bf16[1,6,32,512]{3,2,1,0:T(8,128)(2,1)} %get-tuple-element.20), channel_id=1, source_target_pairs={{16,0},{32,16},{48,32},{64,48},{80,64},{96,80},{112,96},{17,1},{33... | collective-permute-start | bytes 589832 | tf_op jit(solution)/shard_map/ppermute | solution.py:15
  158.1 17.6 %collective-permute-start.6 = (bf16[1,6,32,512]{3,2,1,0:T(8,128)(2,1)}, bf16[1,6,32,512]{3,2,1,0:T(8,128)(2,1)}, u32[]{:S(2)}, u32[]{:S(2)}) collective-permute-start(bf16[1,6,32,512]{3,2,1,0:T(8,128)(2,1)} %get-tuple-element.19), channel_id=1, source_target_pairs={{0,16},{16,32},{32,48},{48,64},{64,80},{80,96},{96,112},{1,17},{17... | collective-permute-start | bytes 589832 | tf_op jit(solution)/shard_map/ppermute | solution.py:14
  162.2 14.9 %copy-start.37 = (s32[128]{0:T(128)S(1)}, s32[128]{0:T(128)}, u32[]{:S(2)}) copy-start(s32[128]{0:T(128)} %fusion.48) | copy-start | bytes 1540
  (29 other events, 101.2 us)
where the time goes:
time: 186 us; the launch traced here: 185 us
  local copies, waits for them, and re-layouts  52.6 us (28%)
  other arithmetic  50.5 us (27%)
  starting transfers between devices  42.9 us (23%)
  matrix products  36.5 us (20%)
  between operations  1.98 us (1%)
    unnamed x91, local copies, waits for them, and re-layouts  18.9 us
    ppermute x4, starting transfers between devices, padded(): after = lax.ppermute(initial, axis, down)  16.5 us
    scatter-add x1, other arithmetic, local_layer(): sender_rows = table[sender_slot]  14 us
    scatter-add x1, other arithmetic, local_layer(): receiver_rows = node_wide[receiver]  13.4 us
    all_to_all x1, starting transfers between devices, per_device(): lax.all_to_all(outgoing, ('lat', 'lon'), split_axis=0, concat_axis=0, til...  12 us
    all_to_all x1, starting transfers between devices, per_device(): lax.all_to_all(slot_grad.reshape(lat_size * lon_size, slots, width).astyp...  9.4 us
    gather x1, local copies, waits for them, and re-layouts, local_layer(): receiver_rows = node_wide[receiver]  9.23 us
    gather x1, local copies, waits for them, and re-layouts, local_layer(): sender_rows = table[sender_slot]  9.21 us
  transfers between devices with their start and end apart: 10, of which 0 were waited for; matrix products, arithmetic and copies ran while one was open for 34% of the time, Pallas kernels for 0%

commit v1 on v0

v1 whole, which is shorter than its diff:
```python
import functools

import jax
import jax.numpy as jnp
from jax import lax
from jax.experimental import pallas as pl
from jax.experimental.pallas import tpu as pltpu
from jax.sharding import PartitionSpec as P

BF = jnp.bfloat16
F32 = jnp.float32
MESH = pl.DeviceIdType.MESH
N_LAT, N_LON = 8, 16
DEVICES = 128
D = 512
NODE = 256
EDGE = 2048
HALO = 32
CAP = 4
FAR = DEVICES * CAP
BORDER = 16 * HALO
TILE = 256
LIMIT = 56 * 1024 * 1024

def _owner(row):
    return (-1, 1) if row == 0 else (1, 0) if row == 3 else (0, row - 1)


CELLS = []
for _r in range(4):
    for _s in range(4):
        _di, _a = _owner(_r)
        _dj, _b = _owner(_s)
        if _di or _dj:
            CELLS.append((_r * 4 + _s, _di, _dj, _a, _b))


def dot(a, b):
    return jnp.dot(a, b, preferred_element_type=F32)


def dot_t(a, b):
    return lax.dot_general(a, b, (((1,), (1,)), ((), ())), preferred_element_type=F32)


def column(row):
    return jnp.transpose(jnp.broadcast_to(row, (128, 128)))


def onehot_cols(col, base, width):
    lane = lax.broadcasted_iota(jnp.int32, col.shape, 1)
    parts = [
        jnp.where(col == lane + (base + k), 1.0, 0.0).astype(BF) for k in range(0, width, 128)
    ]
    return jnp.concatenate(parts, axis=1)


def onehot_rows(rows, base, height):
    parts = []
    for row in rows:
        place = lax.broadcasted_iota(jnp.int32, (height, 128), 0) + base
        parts.append(jnp.where(place == row, 1.0, 0.0).astype(BF))
    return jnp.concatenate(parts, axis=1) if len(parts) > 1 else parts[0]


def position():
    return lax.axis_index("lat"), lax.axis_index("lon")


def greet(lat, lon):
    me = lat * N_LON + lon
    barrier = pltpu.get_barrier_semaphore()

    def one(step, carry):
        peer = lax.rem(me + step, DEVICES)
        pl.semaphore_signal(
            barrier,
            inc=1,
            device_id=(peer // N_LON, lax.rem(peer, N_LON)),
            device_id_type=MESH,
        )
        return carry

    lax.fori_loop(1, DEVICES, one, 0)
    return barrier


def scatter_far(lat, lon, source, target, send_sem, recv_sem):
    me = lat * N_LON + lon

    def one(step, carry):
        peer = lax.rem(me + step, DEVICES)
        pltpu.make_async_remote_copy(
            src_ref=source.at[peer],
            dst_ref=target.at[me],
            send_sem=send_sem,
            recv_sem=recv_sem,
            device_id=(peer // N_LON, lax.rem(peer, N_LON)),
            device_id_type=MESH,
        ).start()
        return carry

    lax.fori_loop(1, DEVICES, one, 0)


def far_waits(source, target, send_sem, recv_sem):
    some = pl.ds(0, DEVICES - 1)
    pltpu.make_async_copy(source.at[some], target.at[some], recv_sem).wait()
    pltpu.make_async_copy(source.at[some], target.at[some], send_sem).wait()


def around(lat, lon, di, dj):
    return (lax.rem(lat + di + N_LAT, N_LAT), lax.rem(lon + dj + N_LON, N_LON))


def fetch_kernel(
    node, slots, groups, border, far, wide, out, send_sem, recv_sem, own_sem, cell_send, cell_recv
):
    lat, lon = position()
    me = lat * N_LON + lon
    barrier = greet(lat, lon)
    rows = dot(onehot_cols(column(groups[...]), 0, NODE), node[...]).astype(BF)
    for a in range(2):
        for b in range(2):
            g = 2 * a + b
            border[(a + 1) * 4 + b + 1] = rows[g * HALO : (g + 1) * HALO]
    for block in range(FAR // 128):
        rows = dot(onehot_cols(column(slots[block : block + 1, :]), 0, NODE), node[...])
        for k in range(4):
            wide[pl.ds(512 * block + k, 128, stride=4), :] = rows[:, 128 * k : 128 * k + 128]
    out[...] = wide[...].astype(BF).reshape(DEVICES, 16, 128)
    pl.semaphore_wait(barrier, DEVICES - 1)
    copies = []
    for i, (cell, di, dj, a, b) in enumerate(CELLS):
        copy = pltpu.make_async_remote_copy(
            src_ref=border.at[(a + 1) * 4 + b + 1],
            dst_ref=border.at[cell],
            send_sem=cell_send.at[i],
            recv_sem=cell_recv.at[i],
            device_id=around(lat, lon, -di, -dj),
            device_id_type=MESH,
        )
        copy.start()
        copies.append(copy)
    scatter_far(lat, lon, out, far, send_sem, recv_sem)
    own = pltpu.make_async_copy(out.at[me], far.at[me], own_sem)
    own.start()
    own.wait()
    for copy in copies:
        copy.wait()
    far_waits(out, far, send_sem, recv_sem)


def return_kernel(
    partial, border_grad, far_grad, slots, groups, total,
    cells, far, wide, send_sem, recv_sem, own_sem, cell_send, cell_recv
):
    lat, lon = position()
    me = lat * N_LON + lon
    barrier = greet(lat, lon)
    pl.semaphore_wait(barrier, DEVICES - 1)
    copies = []
    for i, (cell, di, dj, a, b) in enumerate(CELLS):
        kind = 2 * abs(di) + abs(dj) - 1
        copy = pltpu.make_async_remote_copy(
            src_ref=border_grad.at[cell],
            dst_ref=cells.at[kind * 4 + 2 * a + b],
            send_sem=cell_send.at[i],
            recv_sem=cell_recv.at[i],
            device_id=around(lat, lon, di, dj),
            device_id_type=MESH,
        )
        copy.start()
        copies.append(copy)
    scatter_far(lat, lon, far_grad, far, send_sem, recv_sem)
    own = pltpu.make_async_copy(far_grad.at[me], far.at[me], own_sem)
    own.start()
    own.wait()
    for copy in copies:
        copy.wait()
    picked = onehot_rows([groups[...]], 0, NODE)
    summed = partial[...]
    for kind in range(3):
        summed = summed + dot(picked, cells[4 * kind : 4 * kind + 4].reshape(128, D))
    far_waits(far_grad, far, send_sem, recv_sem)
    wide[...] = far[...].reshape(FAR * 4, 128).astype(F32)
    returned = jnp.concatenate(
        [wide[pl.ds(k, FAR, stride=4), :].astype(BF) for k in range(4)], axis=1
    )
    lists = onehot_rows([slots[i : i + 1, :] for i in range(FAR // 128)], 0, NODE)
    total[...] = summed + dot(lists, returned)


def silu_parts(pre):
    sig = 1.0 / (1.0 + jnp.exp(-pre))
    value = pre * sig
    return value, sig + value * (1.0 - sig)


def normal(values):
    mean = jnp.mean(values, -1, keepdims=True)
    centred = values - mean
    var = jnp.mean(centred * centred, -1, keepdims=True)
    return centred, lax.rsqrt(var + 1e-05)


def layer_kernel(
    count, sender, receiver, groups, node, border, far, node_cot,
    hidden_bias, message_bias, edge_scales, node_bias, update_bias, node_scales,
    edge_h, cot_h, we_h, ws_h, wr_h, wm_h, wself_h, wsum_h, wu_h,
    edge_out_h, grad_out_h, node_out, partial, border_grad, far_grad,
    edge, cot, we, ws, wr, wm, wself, wsum, wu,
    edge_out, grad_out, wide, table, rproj, scol, rcol, xhat, slope, message, dpre, rstd, dsummed,
    in_sems, out_sems, grad_sems,
):
    loads = {}
    for i, (name, src, dst) in enumerate(
        (
            ("ws", ws_h, ws), ("wr", wr_h, wr), ("we", we_h, we), ("edge", edge_h, edge),
            ("wm", wm_h, wm), ("wself", wself_h, wself), ("wsum", wsum_h, wsum),
            ("wu", wu_h, wu), ("cot", cot_h, cot),
        )
    ):
        loads[name] = pltpu.make_async_copy(src, dst, in_sems.at[i])
        loads[name].start()
    for j in range(EDGE // 128):
        at = pl.ds(128 * j, 128)
        scol[at, :] = column(sender[j : j + 1, :])
        rcol[at, :] = column(receiver[j : j + 1, :])
    wide[...] = far[...].reshape(FAR * 4, 128).astype(F32)
    loads["ws"].wait()
    table[0:NODE] = dot(node[...], ws[...]).astype(BF)
    for h in range(2):
        at = pl.ds(NODE + 256 * h, 256)
        table[at] = dot(border[8 * h : 8 * h + 8].reshape(256, D), ws[...]).astype(BF)
    for h in range(2):
        rows = jnp.concatenate(
            [wide[pl.ds(1024 * h + k, 256, stride=4), :].astype(BF) for k in range(4)], axis=1
        )
        table[pl.ds(NODE + BORDER + 256 * h, 256)] = dot(rows, ws[...]).astype(BF)
    loads["wr"].wait()
    rproj[...] = (dot(node[...], wr[...]) + hidden_bias[...]).astype(BF)
    loads["we"].wait()
    loads["edge"].wait()
    loads["wm"].wait()
    live_edges = count[0]

    def forward(i, carry):
        at = pl.ds(pl.multiple_of(i * TILE, TILE), TILE)
        pre = (
            dot(edge[at, :], we[...])
            + dot(onehot_cols(scol[at, :], 0, NODE + BORDER + FAR), table[...])
            + dot(onehot_cols(rcol[at, :], 0, NODE), rproj[...])
        )
        value, grad = silu_parts(pre)
        slope[at, :] = grad.astype(BF)
        centred, scale = normal(dot(value.astype(BF), wm[...]) + message_bias[...])
        place = lax.broadcasted_iota(jnp.int32, (TILE, 1), 0) + i * TILE
        scale = jnp.where(place < live_edges, scale, 0.0)
        rstd[at, :] = scale
        hat = centred * scale
        xhat[at, :] = hat.astype(BF)
        said = hat * edge_scales[...]
        message[at, :] = said.astype(BF)
        edge_out[at, :] = (edge[at, :].astype(F32) + said).astype(BF)
        pltpu.make_async_copy(edge_out.at[at, :], edge_out_h.at[at, :], out_sems.at[i]).start()
        return carry

    lax.fori_loop(0, EDGE // TILE, forward, 0)

    receivers = [receiver[j : j + 1, :] for j in range(EDGE // 128)]
    summed = dot(onehot_rows(receivers, 0, NODE), message[...]).astype(BF)
    loads["wself"].wait()
    loads["wsum"].wait()
    value, grad = silu_parts(
        dot(node[...], wself[...]) + dot(summed, wsum[...]) + node_bias[...]
    )
    loads["wu"].wait()
    centred, scale = normal(dot(value.astype(BF), wu[...]) + update_bias[...])
    hat = centred * scale
    node_out[...] = (node[...].astype(F32) + hat * node_scales[...]).astype(BF)
    upper = node_cot[...].astype(F32)
    g = upper * node_scales[...]
    back = scale * (
        g - jnp.mean(g, -1, keepdims=True) - hat * jnp.mean(g * hat, -1, keepdims=True)
    )
    inner = (dot_t(back.astype(BF), wu[...]) * grad).astype(BF)
    dsummed[...] = dot_t(inner, wsum[...]).astype(BF)
    partial[...] = upper + dot_t(inner, wself[...])
    loads["cot"].wait()

    def backward(i, carry):
        at = pl.ds(pl.multiple_of(i * TILE, TILE), TILE)
        upper = cot[at, :].astype(F32)
        g = (upper + dot(onehot_cols(rcol[at, :], 0, NODE), dsummed[...])) * edge_scales[...]
        hat = xhat[at, :].astype(F32)
        back = rstd[at, :] * (
            g - jnp.mean(g, -1, keepdims=True) - hat * jnp.mean(g * hat, -1, keepdims=True)
        )
        inner = (dot_t(back.astype(BF), wm[...]) * slope[at, :].astype(F32)).astype(BF)
        dpre[at, :] = inner
        grad_out[at, :] = upper + dot_t(inner, we[...])
        pltpu.make_async_copy(grad_out.at[at, :], grad_out_h.at[at, :], grad_sems.at[i]).start()
        return carry

    lax.fori_loop(0, EDGE // TILE, backward, 0)

    senders = [sender[j : j + 1, :] for j in range(EDGE // 128)]

    def table_grad(base):
        rows = dot(onehot_rows(senders, base, 256), dpre[...]).astype(BF)
        return dot_t(rows, ws[...])

    for h in range(2):
        rows = table_grad(NODE + BORDER + 256 * h)
        for k in range(4):
            wide[pl.ds(1024 * h + k, 256, stride=4), :] = rows[:, 128 * k : 128 * k + 128]
    far_grad[...] = wide[...].astype(BF).reshape(DEVICES, 16, 128)
    for h in range(2):
        border_grad[8 * h : 8 * h + 8] = table_grad(NODE + 256 * h).astype(BF).reshape(8, HALO, D)
    center = jnp.concatenate([border_grad[cell] for cell in (5, 6, 9, 10)], axis=0)
    received = dot(onehot_rows(receivers, 0, NODE), dpre[...]).astype(BF)
    partial[...] += (
        table_grad(0)
        + dot_t(received, wr[...])
        + dot(onehot_rows([groups[...]], 0, NODE), center)
    )
    for i in range(EDGE // TILE):
        at = pl.ds(i * TILE, TILE)
        pltpu.make_async_copy(edge_out.at[at, :], edge_out_h.at[at, :], out_sems.at[i]).wait()
        pltpu.make_async_copy(grad_out.at[at, :], grad_out_h.at[at, :], grad_sems.at[i]).wait()


def vmem(count):
    return [pl.BlockSpec(memory_space=pltpu.VMEM)] * count


def per_device(
    node_latent, edge_latent, sender_slot, receiver, border_list, send_list, edge_count,
    edge_weight, sender_weight, receiver_weight, hidden_bias, message_weight, message_bias,
    edge_scales, self_weight, summed_weight, node_bias, update_weight, update_bias, node_scales,
    node_cotangent, edge_cotangent,
):
    groups = border_list.reshape(1, 4 * HALO)
    slots = send_list.reshape(FAR // 128, 128)
    sems = pltpu.SemaphoreType.DMA
    chunks = jax.ShapeDtypeStruct((DEVICES, 16, 128), BF)
    cells = jax.ShapeDtypeStruct((16, HALO, D), BF)
    border, far = pl.pallas_call(
        fetch_kernel,
        out_shape=(cells, chunks),
        in_specs=vmem(3),
        out_specs=tuple(vmem(2)),
        scratch_shapes=[
            pltpu.VMEM((FAR * 4, 128), F32),
            pltpu.VMEM((DEVICES, 16, 128), BF),
            sems, sems, sems, sems((12,)), sems((12,)),
        ],
        compiler_params=pltpu.CompilerParams(
            collective_id=0, has_side_effects=True, vmem_limit_bytes=LIMIT
        ),
        name="fetch",
    )(node_latent, slots, groups)

    weight = pltpu.VMEM((D, D), BF)
    half = pltpu.VMEM((EDGE, D), BF)
    any_space = pl.BlockSpec(memory_space=pl.ANY)
    vector = lambda v: v.reshape(1, D)
    edge_result, edge_grad, node_result, partial, border_grad, far_grad = pl.pallas_call(
        layer_kernel,
        out_shape=(
            jax.ShapeDtypeStruct((EDGE, D), BF),
            jax.ShapeDtypeStruct((EDGE, D), F32),
            jax.ShapeDtypeStruct((NODE, D), BF),
            jax.ShapeDtypeStruct((NODE, D), F32),
            cells,
            chunks,
        ),
        in_specs=[pl.BlockSpec(memory_space=pltpu.SMEM)] + vmem(13) + [any_space] * 9,
        out_specs=tuple([any_space] * 2 + vmem(4)),
        scratch_shapes=[half, half]
        + [weight] * 7
        + [
            half,
            pltpu.VMEM((EDGE, D), F32),
            pltpu.VMEM((FAR * 4, 128), F32),
            pltpu.VMEM((NODE + BORDER + FAR, D), BF),
            pltpu.VMEM((NODE, D), BF),
            pltpu.VMEM((EDGE, 128), jnp.int32),
            pltpu.VMEM((EDGE, 128), jnp.int32),
            half, half, half, half,
            pltpu.VMEM((EDGE, 1), F32),
            pltpu.VMEM((NODE, D), BF),
            sems((9,)),
            sems((EDGE // TILE,)),
            sems((EDGE // TILE,)),
        ],
        compiler_params=pltpu.CompilerParams(vmem_limit_bytes=LIMIT),
        name="layer",
    )(
        edge_count, sender_slot.reshape(EDGE // 128, 128), receiver.reshape(EDGE // 128, 128),
        groups, node_latent, border, far, node_cotangent,
        vector(hidden_bias), vector(message_bias), vector(edge_scales),
        vector(node_bias), vector(update_bias), vector(node_scales),
        edge_latent, edge_cotangent, edge_weight, sender_weight, receiver_weight,
        message_weight, self_weight, summed_weight, update_weight,
    )

    node_grad = pl.pallas_call(
        return_kernel,
        out_shape=jax.ShapeDtypeStruct((NODE, D), F32),
        in_specs=vmem(5),
        out_specs=vmem(1)[0],
        scratch_shapes=[
            pltpu.VMEM((12, HALO, D), BF),
            pltpu.VMEM((DEVICES, 16, 128), BF),
            pltpu.VMEM((FAR * 4, 128), F32),
            sems, sems, sems, sems((12,)), sems((12,)),
        ],
        compiler_params=pltpu.CompilerParams(
            collective_id=1, has_side_effects=True, vmem_limit_bytes=LIMIT
        ),
        name="give_back",
    )(partial, border_grad, far_grad, slots, groups)
    return node_result, edge_result, node_grad, edge_grad


def solution(mesh):
    both = ("lat", "lon")
    placed = (
        P(both, None), P(both, None), P(both), P(both), P(both, None, None, None),
        P(both, None, None), P(both),
        P(), P(), P(), P(), P(), P(), P(), P(), P(), P(), P(), P(), P(),
        P(both, None), P(both, None),
    )
    return jax.shard_map(
        per_device,
        mesh=mesh,
        in_specs=placed,
        out_specs=(P(both, None),) * 4,
        check_vma=False,
    )
```

time: 186 us -> 81 us (0.44)
  Pallas kernels: 0 us -> 74.8 us
  other arithmetic: 50.5 us -> 0 us
  local copies, waits for them, and re-layouts: 52.6 us -> 4.6 us
  starting transfers between devices: 42.9 us -> 0 us
  matrix products: 36.5 us -> 0 us
    pallas_call x0 -> x3, Pallas kernels: none -> 74.8 us  [the longest x1 28.9 us: per_device(): pl.pallas_call(layer_kernel, out_shape=(jax.ShapeDtypeStruct((EDGE, D), B...]
    dot_general x14 -> x0, matrix products: 36.5 us -> none  [the longest x2 6.5 us: local_layer(): jnp.dot(edge_widened.astype(jnp.bfloat16), edge_weight, preferred_element...]
    scatter-add x4 -> x0, other arithmetic: 32.8 us -> none  [the longest x1 14 us: local_layer(): sender_rows = table[sender_slot]]
    gather x5 -> x0, local copies, waits for them, and re-layouts: 25 us -> none  [the longest x1 9.23 us: local_layer(): receiver_rows = node_wide[receiver]]
    ppermute x8 -> x0, starting transfers between devices: 21.5 us -> none  [the longest x4 16.5 us: padded(): after = lax.ppermute(initial, axis, down)]
    all_to_all x2 -> x0, starting transfers between devices: 21.4 us -> none  [the longest x1 12 us: per_device(): lax.all_to_all(outgoing, ('lat', 'lon'), split_axis=0, concat_axis=0, til...]
    unnamed x91 -> x2, local copies, waits for them, and re-layouts: 18.9 us -> 2.66 us
    reduce_sum x5 -> x0, other arithmetic: 8.28 us -> none  [the longest x2 7.33 us: layer_norm(): centred = values - average]
  transfers between devices with their start and end apart: 10 -> 0, of which waited for: 0 -> 0; matrix products, arithmetic and copies ran while one was open for 34% -> 0% of each run, Pallas kernels for 0% -> 0%
where the time goes in v1:
time: 81 us; the launch traced here: 80.7 us
  Pallas kernels  74.8 us (92%)
  local copies, waits for them, and re-layouts  4.6 us (6%)
  between operations  1.3 us (2%)
    pallas_call x1, Pallas kernels, per_device(): pl.pallas_call(layer_kernel, out_shape=(jax.ShapeDtypeStruct((EDGE, D), B...  28.9 us
    pallas_call x1, Pallas kernels, per_device(): pl.pallas_call(fetch_kernel, out_shape=(cells, chunks), in_specs=vmem(3),...  24.4 us
    pallas_call x1, Pallas kernels, per_device(): pl.pallas_call(return_kernel, out_shape=jax.ShapeDtypeStruct((NODE, D), F...  21.5 us
    unnamed x2, local copies, waits for them, and re-layouts  2.66 us

profile of v1, /device:TPU:1, one launch (start us, length us, event | category | flops | bytes accessed | tf_op | source)
XLA Modules:
  0.0 80.7 jit_solution(17202492624277682627)
XLA Ops:
  1.3 1.2 %reshape.40.groups = s32[1,128]{1,0:T(1,128)} reshape(s32[1,2,2,32]{3,2,1,0:T(2,128)} %param.26) | data formatting | bytes 1024 | tf_op jit(solution)/shard_map/reshape | solution.py:344
  2.5 0.8 copy.27
  3.3 0.7 reshape.41.slots
  4.0 24.4 %fetch.1 = (bf16[16,32,512]{2,1,0:T(8,128)(2,1)}, bf16[128,16,128]{2,1,0:T(8,128)(2,1)}) custom-call(bf16[256,512]{1,0:T(8,128)(2,1)} %node.3, s32[4,128]{1,0:T(4,128)} %reshape.41.slots, s32[1,128]{1,0:T(1,128)} %reshape.40.groups), custom_call_target="tpu_custom_call" | custom-call | tf_op jit(solution)/shard_map/fetch/pallas_call | solution.py:349
  28.4 28.9 %layer.1 = (bf16[2048,512]{1,0:T(8,128)(2,1)}, f32[2048,512]{1,0:T(8,128)}, bf16[256,512]{1,0:T(8,128)(2,1)}, f32[256,512]{1,0:T(8,128)}, bf16[16,32,512]{2,1,0:T(8,128)(2,1)}, /*index=5*/bf16[128,16,128]{2,1,0:T(8,128)(2,1)}) custom-call(s32[1]{0:T(128)S(6)} %copy.29.count, s32[16,128]{1,0:T(8,128)} %bitcast.8, s32[16,128]{1,0:T(8,128)} %bitcast.9, ...), custom_call_target="tpu_custom_call" | custom-call | tf_op jit(solution)/shard_map/layer/pallas_call | solution.py:369
  57.3 21.5 %give_back.1 = f32[256,512]{1,0:T(8,128)} custom-call(f32[256,512]{1,0:T(8,128)} %get-tuple-element.16.partial, bf16[16,32,512]{2,1,0:T(8,128)(2,1)} %get-tuple-element.17.border_grad, bf16[128,16,128]{2,1,0:T(8,128)(2,1)} %get-tuple-element.18.far_grad, s32[4,128]{1,0:T(4,128)} %reshape.41.slots, s32[1,128]{1,0:T(1,128)} %reshape.40.groups), custom_call_target="tpu_custom_call" | custom-call | tf_op jit(solution)/shard_map/give_back/pallas_call | solution.py:409
  78.8 1.9 %copy.30 = f32[256,512]{1,0:T(8,128)} copy(f32[256,512]{1,0:T(8,128)} %give_back.1) | data formatting | bytes 1048576

commit v2 on v1

v2 whole, which is shorter than its diff:
```python
import functools

import jax
import jax.numpy as jnp
from jax import lax
from jax.experimental import pallas as pl
from jax.experimental.pallas import tpu as pltpu
from jax.sharding import PartitionSpec as P

BF = jnp.bfloat16
F32 = jnp.float32
MESH = pl.DeviceIdType.MESH
N_LAT, N_LON = 8, 16
DEVICES = 128
D = 512
NODE = 256
EDGE = 2048
HALO = 32
CAP = 4
FAR = DEVICES * CAP
BORDER = 16 * HALO
TILE = 512
LIMIT = 44 * 1024 * 1024

def _owner(row):
    return (-1, 1) if row == 0 else (1, 0) if row == 3 else (0, row - 1)


CELLS = []
for _r in range(4):
    for _s in range(4):
        _di, _a = _owner(_r)
        _dj, _b = _owner(_s)
        if _di or _dj:
            CELLS.append((_r * 4 + _s, _di, _dj, _a, _b))


def dot(a, b):
    return jnp.dot(a, b, preferred_element_type=F32)


def dot_t(a, b):
    return lax.dot_general(a, b, (((1,), (1,)), ((), ())), preferred_element_type=F32)


def column(row):
    return jnp.transpose(jnp.broadcast_to(row, (128, 128)))


def onehot_cols(col, base, width):
    lane = lax.broadcasted_iota(jnp.int32, col.shape, 1)
    parts = [
        jnp.where(col == lane + (base + k), 1.0, 0.0).astype(BF) for k in range(0, width, 128)
    ]
    return jnp.concatenate(parts, axis=1)


def onehot_rows(rows, base, height):
    parts = []
    for row in rows:
        place = lax.broadcasted_iota(jnp.int32, (height, 128), 0) + base
        parts.append(jnp.where(place == row, 1.0, 0.0).astype(BF))
    return jnp.concatenate(parts, axis=1) if len(parts) > 1 else parts[0]


def position():
    return lax.axis_index("lat"), lax.axis_index("lon")


def greet(lat, lon):
    me = lat * N_LON + lon
    barrier = pltpu.get_barrier_semaphore()

    def one(step, carry):
        peer = lax.rem(me + step, DEVICES)
        pl.semaphore_signal(
            barrier,
            inc=1,
            device_id=(peer // N_LON, lax.rem(peer, N_LON)),
            device_id_type=MESH,
        )
        return carry

    lax.fori_loop(1, DEVICES, one, 0)
    return barrier


def scatter_far(lat, lon, source, target, send_sem, recv_sem):
    me = lat * N_LON + lon

    def one(step, carry):
        peer = lax.rem(me + step, DEVICES)
        pltpu.make_async_remote_copy(
            src_ref=source.at[peer],
            dst_ref=target.at[me],
            send_sem=send_sem,
            recv_sem=recv_sem,
            device_id=(peer // N_LON, lax.rem(peer, N_LON)),
            device_id_type=MESH,
        ).start()
        return carry

    lax.fori_loop(1, DEVICES, one, 0)


def far_waits(source, target, send_sem, recv_sem):
    some = pl.ds(0, DEVICES - 1)
    pltpu.make_async_copy(source.at[some], target.at[some], recv_sem).wait()
    pltpu.make_async_copy(source.at[some], target.at[some], send_sem).wait()


def around(lat, lon, di, dj):
    return (lax.rem(lat + di + N_LAT, N_LAT), lax.rem(lon + dj + N_LON, N_LON))


def group_row(groups):
    return jnp.concatenate([groups[0, a, b : b + 1, :] for a in range(2) for b in range(2)], axis=1)


def columns(rows, target):
    for j in range(EDGE // 128):
        target[128 * j : 128 * j + 128, :] = column(rows[j : j + 1, :])


def silu_parts(pre):
    sig = 1.0 / (1.0 + jnp.exp(-pre))
    value = pre * sig
    return value, sig + value * (1.0 - sig)


def normal(values):
    mean = jnp.mean(values, -1, keepdims=True)
    centred = values - mean
    var = jnp.mean(centred * centred, -1, keepdims=True)
    return centred, lax.rsqrt(var + 1e-05)


def send_cells(lat, lon, source, target, inward, cell_send, cell_recv):
    copies = []
    for i, (cell, di, dj, a, b) in enumerate(CELLS):
        if inward:
            kind = 2 * abs(di) + abs(dj) - 1
            src, dst, peer = source.at[cell], target.at[kind * 4 + 2 * a + b], (di, dj)
        else:
            src, dst, peer = source.at[(a + 1) * 4 + b + 1], target.at[cell], (-di, -dj)
        copy = pltpu.make_async_remote_copy(
            src_ref=src,
            dst_ref=dst,
            send_sem=cell_send.at[i],
            recv_sem=cell_recv.at[i],
            device_id=around(lat, lon, *peer),
            device_id_type=MESH,
        )
        copy.start()
        copies.append(copy)
    return copies


def layer_kernel(
    count, node_h, groups_h, slots_h, ws_h, wr_h, hidden_bias_h, sender_h, receiver_h, we_h, edge_h,
    wm_h, message_bias_h, edge_scales_h, wself_h, wsum_h, node_bias_h, wu_h, update_bias_h,
    node_scales_h, node_cot_h, cot_h,
    edge_out_h, dpre_h, node_out_h, total_h,
    node, groups, slots, ws, wr, hidden_bias, sender, receiver, we, edge,
    wm, message_bias, edge_scales, wself, wsum, node_bias, wu, update_bias,
    node_scales, node_cot, cot,
    border, wide, out, far, table, rproj, scol, rcol, pre,
    edge_out, xhat, slope, message, dpre, rstd, dsummed, node_out, total,
    border_grad, far_grad, far_back, cells_back,
    in_sems, edge_sems, dpre_sems, node_sems, far_sems, cell_send, cell_recv, back_send, back_recv,
):
    lat, lon = position()
    me = lat * N_LON + lon
    loads = []
    for i, (src, dst) in enumerate(
        (
            (node_h, node), (groups_h, groups), (slots_h, slots), (ws_h, ws), (wr_h, wr),
            (hidden_bias_h, hidden_bias), (sender_h, sender), (receiver_h, receiver),
            (we_h, we), (edge_h, edge), (wm_h, wm), (message_bias_h, message_bias),
            (edge_scales_h, edge_scales), (wself_h, wself), (wsum_h, wsum),
            (node_bias_h, node_bias), (wu_h, wu), (update_bias_h, update_bias),
            (node_scales_h, node_scales), (node_cot_h, node_cot), (cot_h, cot),
        )
    ):
        load = pltpu.make_async_copy(src, dst, in_sems.at[i])
        load.start()
        loads.append(load)
    barrier = greet(lat, lon)

    def arrived(first, last):
        for load in loads[first:last]:
            load.wait()

    arrived(0, 3)
    rows = dot(onehot_cols(column(group_row(groups)), 0, NODE), node[...]).astype(BF)
    for a in range(2):
        for b in range(2):
            g = 2 * a + b
            border[(a + 1) * 4 + b + 1] = rows[g * HALO : (g + 1) * HALO]
    for c in range(CAP):
        rows = dot(onehot_cols(column(slots[0, c : c + 1, :]), 0, NODE), node[...])
        for k in range(4):
            wide[pl.ds(4 * c + k, DEVICES, stride=16), :] = rows[:, 128 * k : 128 * k + 128]
    out[...] = wide[...].astype(BF).reshape(DEVICES, 16, 128)
    pl.semaphore_wait(barrier, DEVICES - 1)
    copies = send_cells(lat, lon, border, border, False, cell_send, cell_recv)
    scatter_far(lat, lon, out, far, far_sems.at[0], far_sems.at[1])
    own = pltpu.make_async_copy(out.at[me], far.at[me], far_sems.at[2])
    own.start()
    arrived(3, 10)
    columns(sender, scol)
    columns(receiver, rcol)
    table[0:NODE] = dot(node[...], ws[...]).astype(BF)
    rproj[...] = (dot(node[...], wr[...]) + hidden_bias[...]).astype(BF)
    for copy in copies:
        copy.wait()
    for h in range(2):
        at = pl.ds(NODE + 256 * h, 256)
        table[at] = dot(border[8 * h : 8 * h + 8].reshape(256, D), ws[...]).astype(BF)

    def near(i, carry):
        at = pl.ds(pl.multiple_of(i * TILE, TILE), TILE)
        pre[at, :] = (
            dot(edge[at, :], we[...])
            + dot(onehot_cols(scol[at, :], 0, NODE + BORDER), table[0 : NODE + BORDER])
            + dot(onehot_cols(rcol[at, :], 0, NODE), rproj[...])
        )
        return carry

    lax.fori_loop(0, EDGE // TILE, near, 0)
    arrived(10, 21)
    own.wait()
    far_waits(out, far, far_sems.at[0], far_sems.at[1])
    wide[...] = far[...].reshape(FAR * 4, 128).astype(F32)
    for h in range(2):
        rows = jnp.concatenate(
            [wide[pl.ds(1024 * h + k, 256, stride=4), :].astype(BF) for k in range(4)], axis=1
        )
        table[pl.ds(NODE + BORDER + 256 * h, 256)] = dot(rows, ws[...]).astype(BF)
    live_edges = count[0]

    def forward(i, carry):
        at = pl.ds(pl.multiple_of(i * TILE, TILE), TILE)
        value, grad = silu_parts(
            pre[at, :]
            + dot(
                onehot_cols(scol[at, :], NODE + BORDER, FAR),
                table[NODE + BORDER : NODE + BORDER + FAR],
            )
        )
        slope[at, :] = grad.astype(BF)
        centred, scale = normal(dot(value.astype(BF), wm[...]) + message_bias[...])
        place = lax.broadcasted_iota(jnp.int32, (TILE, 1), 0) + i * TILE
        scale = jnp.where(place < live_edges, scale, 0.0)
        rstd[at, :] = scale
        hat = centred * scale
        xhat[at, :] = hat.astype(BF)
        said = hat * edge_scales[...]
        message[at, :] = said.astype(BF)
        edge_out[at, :] = (edge[at, :].astype(F32) + said).astype(BF)
        pltpu.make_async_copy(edge_out.at[at, :], edge_out_h.at[at, :], edge_sems.at[i]).start()
        return carry

    lax.fori_loop(0, EDGE // TILE, forward, 0)

    receivers = [receiver[j : j + 1, :] for j in range(EDGE // 128)]
    summed = dot(onehot_rows(receivers, 0, NODE), message[...]).astype(BF)
    value, grad = silu_parts(
        dot(node[...], wself[...]) + dot(summed, wsum[...]) + node_bias[...]
    )
    centred, scale = normal(dot(value.astype(BF), wu[...]) + update_bias[...])
    hat = centred * scale
    node_out[...] = (node[...].astype(F32) + hat * node_scales[...]).astype(BF)
    node_copy = pltpu.make_async_copy(node_out, node_out_h, node_sems.at[0])
    node_copy.start()
    upper = node_cot[...].astype(F32)
    g = upper * node_scales[...]
    back = scale * (
        g - jnp.mean(g, -1, keepdims=True) - hat * jnp.mean(g * hat, -1, keepdims=True)
    )
    inner = (dot_t(back.astype(BF), wu[...]) * grad).astype(BF)
    dsummed[...] = dot_t(inner, wsum[...]).astype(BF)
    total[...] = upper + dot_t(inner, wself[...])

    def backward(i, carry):
        at = pl.ds(pl.multiple_of(i * TILE, TILE), TILE)
        upper = cot[at, :].astype(F32)
        g = (upper + dot(onehot_cols(rcol[at, :], 0, NODE), dsummed[...])) * edge_scales[...]
        hat = xhat[at, :].astype(F32)
        back = rstd[at, :] * (
            g - jnp.mean(g, -1, keepdims=True) - hat * jnp.mean(g * hat, -1, keepdims=True)
        )
        dpre[at, :] = (dot_t(back.astype(BF), wm[...]) * slope[at, :].astype(F32)).astype(BF)
        pltpu.make_async_copy(dpre.at[at, :], dpre_h.at[at, :], dpre_sems.at[i]).start()
        return carry

    lax.fori_loop(0, EDGE // TILE, backward, 0)

    senders = [sender[j : j + 1, :] for j in range(EDGE // 128)]

    def table_grad(base):
        rows = dot(onehot_rows(senders, base, 256), dpre[...]).astype(BF)
        return dot_t(rows, ws[...])

    for h in range(2):
        rows = table_grad(NODE + BORDER + 256 * h)
        for k in range(4):
            wide[pl.ds(1024 * h + k, 256, stride=4), :] = rows[:, 128 * k : 128 * k + 128]
    far_grad[...] = wide[...].astype(BF).reshape(DEVICES, 16, 128)
    scatter_far(lat, lon, far_grad, far_back, far_sems.at[3], far_sems.at[4])
    own = pltpu.make_async_copy(far_grad.at[me], far_back.at[me], far_sems.at[5])
    own.start()
    for h in range(2):
        border_grad[8 * h : 8 * h + 8] = table_grad(NODE + 256 * h).astype(BF).reshape(8, HALO, D)
    copies = send_cells(lat, lon, border_grad, cells_back, True, back_send, back_recv)
    received = dot(onehot_rows(receivers, 0, NODE), dpre[...]).astype(BF)
    picked = onehot_rows([group_row(groups)], 0, NODE)
    center = jnp.concatenate([border_grad[cell] for cell in (5, 6, 9, 10)], axis=0)
    total[...] += table_grad(0) + dot_t(received, wr[...]) + dot(picked, center)
    for copy in copies:
        copy.wait()
    summed = dot(picked, cells_back[0:4].reshape(128, D))
    for kind in (1, 2):
        summed = summed + dot(picked, cells_back[4 * kind : 4 * kind + 4].reshape(128, D))
    total[...] += summed
    own.wait()
    far_waits(far_grad, far_back, far_sems.at[3], far_sems.at[4])
    wide[...] = far_back[...].reshape(FAR * 4, 128).astype(F32)
    returned = jnp.concatenate(
        [
            jnp.concatenate(
                [wide[pl.ds(4 * c + k, DEVICES, stride=16), :].astype(BF) for k in range(4)], axis=1
            )
            for c in range(CAP)
        ],
        axis=0,
    )
    lists = onehot_rows([slots[0, c : c + 1, :] for c in range(CAP)], 0, NODE)
    total[...] += dot(lists, returned)
    total_copy = pltpu.make_async_copy(total, total_h, node_sems.at[1])
    total_copy.start()
    for i in range(EDGE // TILE):
        at = pl.ds(i * TILE, TILE)
        pltpu.make_async_copy(edge_out.at[at, :], edge_out_h.at[at, :], edge_sems.at[i]).wait()
        pltpu.make_async_copy(dpre.at[at, :], dpre_h.at[at, :], dpre_sems.at[i]).wait()
    node_copy.wait()
    total_copy.wait()


def finish_kernel(
    edge_i, node_i, total_i, dpre_h, cot_h, we_h, edge_o, node_o, total_o, grad_o,
    dpre, cot, we, grad, pass_sems, we_sem, dpre_sems, cot_sems, grad_sems,
):
    weight = pltpu.make_async_copy(we_h, we, we_sem)
    weight.start()
    tiles = [pl.ds(i * TILE, TILE) for i in range(EDGE // TILE)]
    loads = []
    for i, at in enumerate(tiles):
        pair = (
            pltpu.make_async_copy(dpre_h.at[at, :], dpre.at[at, :], dpre_sems.at[i]),
            pltpu.make_async_copy(cot_h.at[at, :], cot.at[at, :], cot_sems.at[i]),
        )
        for copy in pair:
            copy.start()
        loads.append(pair)
    passed = [
        pltpu.make_async_copy(src, dst, pass_sems.at[i])
        for i, (src, dst) in enumerate(((edge_i, edge_o), (node_i, node_o), (total_i, total_o)))
    ]
    for copy in passed:
        copy.start()
    weight.wait()
    stores = []
    for i, at in enumerate(tiles):
        for copy in loads[i]:
            copy.wait()
        grad[at, :] = cot[at, :].astype(F32) + dot_t(dpre[at, :], we[...])
        store = pltpu.make_async_copy(grad.at[at, :], grad_o.at[at, :], grad_sems.at[i])
        store.start()
        stores.append(store)
    for copy in passed + stores:
        copy.wait()


def vmem(count):
    return [pl.BlockSpec(memory_space=pltpu.VMEM)] * count


def per_device(
    node_latent, edge_latent, sender_slot, receiver, border_list, send_list, edge_count,
    edge_weight, sender_weight, receiver_weight, hidden_bias, message_weight, message_bias,
    edge_scales, self_weight, summed_weight, node_bias, update_weight, update_bias, node_scales,
    node_cotangent, edge_cotangent,
):
    slots = send_list.transpose(0, 2, 1)
    sender = sender_slot.reshape(EDGE // 128, 128)
    receiver = receiver.reshape(EDGE // 128, 128)
    sems = pltpu.SemaphoreType.DMA
    tiles = sems((EDGE // TILE,))
    cells = pltpu.VMEM((16, HALO, D), BF)
    chunk = pltpu.VMEM((DEVICES, 16, 128), BF)
    wide = pltpu.VMEM((FAR * 4, 128), F32)
    weight = pltpu.VMEM((D, D), BF)
    half = pltpu.VMEM((EDGE, D), BF)
    full = pltpu.VMEM((EDGE, D), F32)
    nodes = pltpu.VMEM((NODE, D), BF)
    column_of = pltpu.VMEM((EDGE, 128), jnp.int32)
    any_space = pl.BlockSpec(memory_space=pl.ANY)
    hbm = pl.BlockSpec(memory_space=pltpu.HBM)
    line = pltpu.VMEM((1, D), F32)
    slot_rows = pltpu.VMEM((EDGE // 128, 128), jnp.int32)
    keep = lambda v: pltpu.with_memory_space_constraint(v, pltpu.HBM)
    vector = lambda v: v.reshape(1, D)
    results = (
        jax.ShapeDtypeStruct((EDGE, D), BF),
        jax.ShapeDtypeStruct((NODE, D), BF),
        jax.ShapeDtypeStruct((NODE, D), F32),
    )
    edges = jax.ShapeDtypeStruct((EDGE, D), BF)
    edge_result, dpre, node_result, node_grad = pl.pallas_call(
        layer_kernel,
        out_shape=(results[0], edges, results[1], results[2]),
        in_specs=[pl.BlockSpec(memory_space=pltpu.SMEM)] + [hbm] * 21,
        out_specs=(any_space,) * 4,
        scratch_shapes=[
            nodes, pltpu.VMEM((1, 2, 2, HALO), jnp.int32), pltpu.VMEM((1, CAP, DEVICES), jnp.int32),
            weight, weight, line, slot_rows, slot_rows, weight, half,
            weight, line, line, weight, weight, line, weight, line, line, nodes, half,
        ]
        + [
            cells, wide, chunk, chunk, pltpu.VMEM((NODE + BORDER + FAR, D), BF), nodes,
            column_of, column_of, full,
            half, half, half, half, half, pltpu.VMEM((EDGE, 1), F32), nodes, nodes,
            pltpu.VMEM((NODE, D), F32),
            cells, chunk, chunk, pltpu.VMEM((12, HALO, D), BF),
            sems((21,)), tiles, tiles, sems((2,)), sems((6,)),
            sems((12,)), sems((12,)), sems((12,)), sems((12,)),
        ],
        compiler_params=pltpu.CompilerParams(
            collective_id=0, has_side_effects=True, vmem_limit_bytes=LIMIT
        ),
        name="layer",
    )(
        edge_count,
        *map(keep, (
        node_latent, border_list, slots, sender_weight, receiver_weight,
        vector(hidden_bias), sender, receiver, edge_weight, edge_latent,
        message_weight, vector(message_bias), vector(edge_scales), self_weight, summed_weight,
        vector(node_bias), update_weight, vector(update_bias), vector(node_scales),
        node_cotangent, edge_cotangent,
        )),
    )
    edge_result, node_result, node_grad, edge_grad = pl.pallas_call(
        finish_kernel,
        out_shape=(*results, jax.ShapeDtypeStruct((EDGE, D), F32)),
        in_specs=[any_space] * 4 + [hbm] * 2,
        out_specs=(any_space,) * 4,
        scratch_shapes=[half, half, weight, full, sems((3,)), sems, tiles, tiles, tiles],
        compiler_params=pltpu.CompilerParams(vmem_limit_bytes=16 * 1024 * 1024),
        name="finish",
    )(edge_result, node_result, node_grad, dpre, keep(edge_cotangent), keep(edge_weight))
    return node_result, edge_result, node_grad, edge_grad


def solution(mesh):
    both = ("lat", "lon")
    placed = (
        P(both, None), P(both, None), P(both), P(both), P(both, None, None, None),
        P(both, None, None), P(both),
        P(), P(), P(), P(), P(), P(), P(), P(), P(), P(), P(), P(), P(),
        P(both, None), P(both, None),
    )
    return jax.shard_map(
        per_device,
        mesh=mesh,
        in_specs=placed,
        out_specs=(P(both, None),) * 4,
        check_vma=False,
    )
```

time: 81 us -> 59.2 us (0.73)
  Pallas kernels: 74.8 us -> 57.7 us
  local copies, waits for them, and re-layouts: 4.6 us -> 0 us
    pallas_call x3 -> x2, Pallas kernels: 74.8 us -> 57.7 us  [the longest x1 53 us: per_device(): pl.pallas_call(layer_kernel, out_shape=(results[0], edges, results[1], re...]
    unnamed x2 -> x0, local copies, waits for them, and re-layouts: 2.66 us -> none
    reshape x2 -> x0, local copies, waits for them, and re-layouts: 1.95 us -> none  [the longest x1 1.24 us: per_device(): groups = border_list.reshape(1, 4 * HALO)]
where the time goes in v2:
time: 59.2 us; the launch traced here: 59 us
  Pallas kernels  57.7 us (97%)
  between operations  1.29 us (2%)
    pallas_call x1, Pallas kernels, per_device(): pl.pallas_call(layer_kernel, out_shape=(results[0], edges, results[1], re...  53 us
    pallas_call x1, Pallas kernels, per_device(): pl.pallas_call(finish_kernel, out_shape=(*results, jax.ShapeDtypeStruct((...  4.66 us

profile of v2, /device:TPU:1, one launch (start us, length us, event | category | flops | bytes accessed | tf_op | source)
XLA Modules:
  0.0 59.0 jit_solution(14559246426768418166)
XLA Ops:
  1.3 53.0 %layer.1 = (bf16[2048,512]{1,0:T(8,128)(2,1)S(1)}, bf16[2048,512]{1,0:T(8,128)(2,1)S(1)}, bf16[256,512]{1,0:T(8,128)(2,1)S(1)}, f32[256,512]{1,0:T(8,128)S(1)}) custom-call(s32[1]{0:T(128)S(6)} %copy.26.count, bf16[256,512]{1,0:T(8,128)(2,1)} %node_h.1, s32[1,2,2,32]{3,2,1,0:T(2,128)} %groups_h.1, s32[1,4,128]{2,1,0:T(4,128)} %bitcast.11, ...), custom_call_target="tpu_custom_call" | custom-call | tf_op jit(solution)/shard_map/layer/pallas_call | solution.py:420
  54.3 4.7 %finish.1 = (bf16[2048,512]{1,0:T(8,128)(2,1)}, bf16[256,512]{1,0:T(8,128)(2,1)}, f32[256,512]{1,0:T(8,128)}, f32[2048,512]{1,0:T(8,128)}) custom-call(bf16[2048,512]{1,0:T(8,128)(2,1)S(1)} %get-tuple-element.12.edge_i, bf16[256,512]{1,0:T(8,128)(2,1)S(1)} %get-tuple-element.13.node_i, f32[256,512]{1,0:T(8,128)S(1)} %get-tuple-element.14.total_i, ...), custom_call_target="tpu_custom_call" | custom-call | tf_op jit(solution)/shard_map/finish/pallas_call | solution.py:453

commit v3 on v2

--- a/solution.py
+++ b/solution.py
@@ -19,8 +19,10 @@
 CAP = 4
 FAR = DEVICES * CAP
 BORDER = 16 * HALO
-TILE = 512
-LIMIT = 44 * 1024 * 1024
+TILE = 1024
+LIMIT = 46 * 1024 * 1024
+OUTER = NODE + 4 * HALO
+REMOTE = 12 * HALO + FAR
 
 def _owner(row):
     return (-1, 1) if row == 0 else (1, 0) if row == 3 else (0, row - 1)
@@ -68,21 +70,24 @@
 
 
 def greet(lat, lon):
-    me = lat * N_LON + lon
     barrier = pltpu.get_barrier_semaphore()
-
-    def one(step, carry):
-        peer = lax.rem(me + step, DEVICES)
-        pl.semaphore_signal(
-            barrier,
-            inc=1,
-            device_id=(peer // N_LON, lax.rem(peer, N_LON)),
-            device_id_type=MESH,
-        )
-        return carry
-
-    lax.fori_loop(1, DEVICES, one, 0)
+    lats = [lax.rem(lat + i, N_LAT) for i in range(N_LAT)]
+    lons = [lax.rem(lon + j, N_LON) for j in range(N_LON)]
+    for j in range(N_LON):
+        for i in range(N_LAT):
+            if i or j:
+                pl.semaphore_signal(
+                    barrier, inc=1, device_id=(lats[i], lons[j]), device_id_type=MESH
+                )
     return barrier
+
+
+def sender_place(slot):
+    place = jnp.where(slot < 608, slot - 224, slot)
+    place = jnp.where(slot < 544, slot + 64, place)
+    place = jnp.where(slot < 480, slot - 160, place)
+    place = jnp.where(slot < 416, slot + 128, place)
+    return jnp.where(slot < NODE, slot, place)
 
 
 def scatter_far(lat, lon, source, target, send_sem, recv_sem):
@@ -103,6 +108,28 @@
     lax.fori_loop(1, DEVICES, one, 0)
 
 
+def scatter_half(lat, lon, half, source, target, send_sem, recv_sem):
+    me = lat * N_LON + lon
+
+    def one(step, carry):
+        peer = 64 * half + lax.rem(me + step, 64)
+
+        @pl.when(peer != me)
+        def _():
+            pltpu.make_async_remote_copy(
+                src_ref=source.at[peer],
+                dst_ref=target.at[me],
+                send_sem=send_sem,
+                recv_sem=recv_sem,
+                device_id=(peer // N_LON, lax.rem(peer, N_LON)),
+                device_id_type=MESH,
+            ).start()
+
+        return carry
+
+    lax.fori_loop(0, 64, one, 0)
+
+
 def far_waits(source, target, send_sem, recv_sem):
     some = pl.ds(0, DEVICES - 1)
     pltpu.make_async_copy(source.at[some], target.at[some], recv_sem).wait()
@@ -123,9 +150,9 @@
 
 
 def silu_parts(pre):
-    sig = 1.0 / (1.0 + jnp.exp(-pre))
+    sig = 0.5 * jnp.tanh(0.5 * pre) + 0.5
     value = pre * sig
-    return value, sig + value * (1.0 - sig)
+    return value, sig + value - value * sig
 
 
 def normal(values):
@@ -135,12 +162,19 @@
     return centred, lax.rsqrt(var + 1e-05)
 
 
+def pipeline(stages, count):
+    for step in range(count + len(stages) - 1):
+        for lag, stage in enumerate(stages):
+            if 0 <= step - lag < count:
+                stage(step - lag)
+
+
 def send_cells(lat, lon, source, target, inward, cell_send, cell_recv):
     copies = []
     for i, (cell, di, dj, a, b) in enumerate(CELLS):
         if inward:
             kind = 2 * abs(di) + abs(dj) - 1
-            src, dst, peer = source.at[cell], target.at[kind * 4 + 2 * a + b], (di, dj)
+            src, dst, peer = source.at[i], target.at[kind * 4 + 2 * a + b], (di, dj)
         else:
             src, dst, peer = source.at[(a + 1) * 4 + b + 1], target.at[cell], (-di, -dj)
         copy = pltpu.make_async_remote_copy(
@@ -160,14 +194,14 @@
     count, node_h, groups_h, slots_h, ws_h, wr_h, hidden_bias_h, sender_h, receiver_h, we_h, edge_h,
     wm_h, message_bias_h, edge_scales_h, wself_h, wsum_h, node_bias_h, wu_h, update_bias_h,
     node_scales_h, node_cot_h, cot_h,
-    edge_out_h, dpre_h, node_out_h, total_h,
+    edge_out_h, grad_h, node_out_h, total_h,
     node, groups, slots, ws, wr, hidden_bias, sender, receiver, we, edge,
     wm, message_bias, edge_scales, wself, wsum, node_bias, wu, update_bias,
     node_scales, node_cot, cot,
     border, wide, out, far, table, rproj, scol, rcol, pre,
-    edge_out, xhat, slope, message, dpre, rstd, dsummed, node_out, total,
-    border_grad, far_grad, far_back, cells_back,
-    in_sems, edge_sems, dpre_sems, node_sems, far_sems, cell_send, cell_recv, back_send, back_recv,
+    hats, slope, rstd, dsummed, node_out, total,
+    border_grad, far_grad, far_back, cells_back, by_receiver, by_sender, to_receiver, to_far,
+    in_sems, edge_sems, grad_sems, node_sems, far_sems, cell_send, cell_recv, back_send, back_recv,
 ):
     lat, lon = position()
     me = lat * N_LON + lon
@@ -182,10 +216,12 @@
             (node_scales_h, node_scales), (node_cot_h, node_cot), (cot_h, cot),
         )
     ):
-        load = pltpu.make_async_copy(src, dst, in_sems.at[i])
+        loads.append(pltpu.make_async_copy(src, dst, in_sems.at[i]))
+    for load in loads[:3]:
         load.start()
-        loads.append(load)
     barrier = greet(lat, lon)
+    for load in loads[3:]:
+        load.start()
 
     def arrived(first, last):
         for load in loads[first:last]:
@@ -203,32 +239,42 @@
             wide[pl.ds(4 * c + k, DEVICES, stride=16), :] = rows[:, 128 * k : 128 * k + 128]
     out[...] = wide[...].astype(BF).reshape(DEVICES, 16, 128)
     pl.semaphore_wait(barrier, DEVICES - 1)
+    scatter_far(lat, lon, out, far, far_sems.at[0], far_sems.at[1])
     copies = send_cells(lat, lon, border, border, False, cell_send, cell_recv)
-    scatter_far(lat, lon, out, far, far_sems.at[0], far_sems.at[1])
     own = pltpu.make_async_copy(out.at[me], far.at[me], far_sems.at[2])
     own.start()
     arrived(3, 10)
+    sender[...] = sender_place(sender[...])
     columns(sender, scol)
     columns(receiver, rcol)
     table[0:NODE] = dot(node[...], ws[...]).astype(BF)
+    center = jnp.concatenate([border[cell] for cell in (5, 6, 9, 10)], axis=0)
+    table[NODE:OUTER] = dot(center, ws[...]).astype(BF)
     rproj[...] = (dot(node[...], wr[...]) + hidden_bias[...]).astype(BF)
+    def near(i, carry):
+        at = pl.ds(pl.multiple_of(i * TILE, TILE), TILE)
+        picked = onehot_cols(rcol[at, :], 0, NODE)
+        by_receiver[at, :] = picked
+        by_sender[at, :] = onehot_cols(scol[at, :], OUTER, REMOTE)
+        pre[at, :] = (
+            dot(edge[at, :], we[...])
+            + dot(onehot_cols(scol[at, :], 0, OUTER), table[0:OUTER])
+            + dot(picked, rproj[...])
+        )
+        return carry
+
+    lax.fori_loop(0, EDGE // TILE, near, 0)
+    for j in range(EDGE // 128):
+        at = pl.ds(128 * j, 128)
+        to_receiver[:, at] = onehot_rows([receiver[j : j + 1, :]], 0, NODE)
+        to_far[:, at] = onehot_rows([sender[j : j + 1, :]], NODE + BORDER, FAR)
+    arrived(10, 21)
+    total[...] = dot(node[...], wself[...]) + node_bias[...]
     for copy in copies:
         copy.wait()
-    for h in range(2):
-        at = pl.ds(NODE + 256 * h, 256)
-        table[at] = dot(border[8 * h : 8 * h + 8].reshape(256, D), ws[...]).astype(BF)
-
-    def near(i, carry):
-        at = pl.ds(pl.multiple_of(i * TILE, TILE), TILE)
-        pre[at, :] = (
-            dot(edge[at, :], we[...])
-            + dot(onehot_cols(scol[at, :], 0, NODE + BORDER), table[0 : NODE + BORDER])
-            + dot(onehot_cols(rcol[at, :], 0, NODE), rproj[...])
-        )
-        return carry
-
-    lax.fori_loop(0, EDGE // TILE, near, 0)
-    arrived(10, 21)
+    cells = [border[0:5], border[7:9], border[11:16]]
+    cells = jnp.concatenate([c.reshape(-1, D) for c in cells], axis=0)
+    table[OUTER : NODE + BORDER] = dot(cells, ws[...]).astype(BF)
     own.wait()
     far_waits(out, far, far_sems.at[0], far_sems.at[1])
     wide[...] = far[...].reshape(FAR * 4, 128).astype(F32)
@@ -239,35 +285,43 @@
         table[pl.ds(NODE + BORDER + 256 * h, 256)] = dot(rows, ws[...]).astype(BF)
     live_edges = count[0]
 
-    def forward(i, carry):
-        at = pl.ds(pl.multiple_of(i * TILE, TILE), TILE)
-        value, grad = silu_parts(
-            pre[at, :]
-            + dot(
-                onehot_cols(scol[at, :], NODE + BORDER, FAR),
-                table[NODE + BORDER : NODE + BORDER + FAR],
-            )
-        )
-        slope[at, :] = grad.astype(BF)
-        centred, scale = normal(dot(value.astype(BF), wm[...]) + message_bias[...])
+    senders = [sender[j : j + 1, :] for j in range(EDGE // 128)]
+    tiles = [pl.ds(i * TILE, TILE) for i in range(EDGE // TILE)]
+    halves = [{} for _ in tiles]
+    summed = jnp.zeros((NODE, D), F32)
+
+    def inputs(i):
+        at = tiles[i]
+        halves[i]["pre"] = pre[at, :] + dot(by_sender[at, :], table[OUTER : OUTER + REMOTE])
+
+    def activate(i):
+        value, grad = silu_parts(halves[i]["pre"])
+        slope[tiles[i], :] = grad.astype(BF)
+        halves[i]["value"] = value.astype(BF)
+
+    def project(i):
+        halves[i]["message"] = dot(halves[i]["value"], wm[...]) + message_bias[...]
+
+    def normalise(i):
+        at = tiles[i]
+        centred, scale = normal(halves[i]["message"])
         place = lax.broadcasted_iota(jnp.int32, (TILE, 1), 0) + i * TILE
         scale = jnp.where(place < live_edges, scale, 0.0)
         rstd[at, :] = scale
         hat = centred * scale
-        xhat[at, :] = hat.astype(BF)
+        hats[at, :] = hat.astype(BF)
         said = hat * edge_scales[...]
-        message[at, :] = said.astype(BF)
-        edge_out[at, :] = (edge[at, :].astype(F32) + said).astype(BF)
-        pltpu.make_async_copy(edge_out.at[at, :], edge_out_h.at[at, :], edge_sems.at[i]).start()
-        return carry
-
-    lax.fori_loop(0, EDGE // TILE, forward, 0)
-
-    receivers = [receiver[j : j + 1, :] for j in range(EDGE // 128)]
-    summed = dot(onehot_rows(receivers, 0, NODE), message[...]).astype(BF)
-    value, grad = silu_parts(
-        dot(node[...], wself[...]) + dot(summed, wsum[...]) + node_bias[...]
-    )
+        halves[i]["said"] = said.astype(BF)
+        edge[at, :] = (edge[at, :].astype(F32) + said).astype(BF)
+        pltpu.make_async_copy(edge.at[at, :], edge_out_h.at[at, :], edge_sems.at[i]).start()
+
+    def gather_sum(i):
+        nonlocal summed
+        summed = summed + dot(to_receiver[:, tiles[i]], halves[i]["said"])
+
+    pipeline((inputs, activate, project, normalise, gather_sum), len(tiles))
+    summed = summed.astype(BF)
+    value, grad = silu_parts(total[...] + dot(summed, wsum[...]))
     centred, scale = normal(dot(value.astype(BF), wu[...]) + update_bias[...])
     hat = centred * scale
     node_out[...] = (node[...].astype(F32) + hat * node_scales[...]).astype(BF)
@@ -282,41 +336,60 @@
     dsummed[...] = dot_t(inner, wsum[...]).astype(BF)
     total[...] = upper + dot_t(inner, wself[...])
 
-    def backward(i, carry):
-        at = pl.ds(pl.multiple_of(i * TILE, TILE), TILE)
-        upper = cot[at, :].astype(F32)
-        g = (upper + dot(onehot_cols(rcol[at, :], 0, NODE), dsummed[...])) * edge_scales[...]
-        hat = xhat[at, :].astype(F32)
+    far_rows = jnp.zeros((FAR, D), F32)
+
+    def spread(i):
+        at = tiles[i]
+        halves[i]["grad"] = dot(by_receiver[at, :], dsummed[...])
+
+    def denormalise(i):
+        at = tiles[i]
+        g = (cot[at, :].astype(F32) + halves[i]["grad"]) * edge_scales[...]
+        hat = hats[at, :].astype(F32)
         back = rstd[at, :] * (
             g - jnp.mean(g, -1, keepdims=True) - hat * jnp.mean(g * hat, -1, keepdims=True)
         )
-        dpre[at, :] = (dot_t(back.astype(BF), wm[...]) * slope[at, :].astype(F32)).astype(BF)
-        pltpu.make_async_copy(dpre.at[at, :], dpre_h.at[at, :], dpre_sems.at[i]).start()
-        return carry
-
-    lax.fori_loop(0, EDGE // TILE, backward, 0)
-
-    senders = [sender[j : j + 1, :] for j in range(EDGE // 128)]
-
-    def table_grad(base):
-        rows = dot(onehot_rows(senders, base, 256), dpre[...]).astype(BF)
-        return dot_t(rows, ws[...])
+        halves[i]["back"] = back.astype(BF)
+
+    def unproject(i):
+        halves[i]["hidden"] = dot_t(halves[i]["back"], wm[...])
+
+    def deactivate(i):
+        at = tiles[i]
+        hats[at, :] = (halves[i]["hidden"] * slope[at, :].astype(F32)).astype(BF)
+
+    def gather_far(i):
+        nonlocal far_rows
+        far_rows = far_rows + dot(to_far[:, tiles[i]], hats[tiles[i], :])
+
+    pipeline((spread, denormalise, unproject, deactivate, gather_far), len(tiles))
+    far_rows = far_rows.astype(BF)
 
     for h in range(2):
-        rows = table_grad(NODE + BORDER + 256 * h)
+        rows = dot_t(far_rows[256 * h : 256 * h + 256], ws[...])
         for k in range(4):
             wide[pl.ds(1024 * h + k, 256, stride=4), :] = rows[:, 128 * k : 128 * k + 128]
-    far_grad[...] = wide[...].astype(BF).reshape(DEVICES, 16, 128)
-    scatter_far(lat, lon, far_grad, far_back, far_sems.at[3], far_sems.at[4])
+        part = wide[1024 * h : 1024 * h + 1024, :].astype(BF)
+        far_grad[64 * h : 64 * h + 64] = part.reshape(64, 16, 128)
+        scatter_half(lat, lon, h, far_grad, far_back, far_sems.at[3], far_sems.at[4])
     own = pltpu.make_async_copy(far_grad.at[me], far_back.at[me], far_sems.at[5])
     own.start()
-    for h in range(2):
-        border_grad[8 * h : 8 * h + 8] = table_grad(NODE + 256 * h).astype(BF).reshape(8, HALO, D)
+    rows = dot(onehot_rows(senders, OUTER, 12 * HALO), hats[...]).astype(BF)
+    border_grad[...] = dot_t(rows, ws[...]).astype(BF).reshape(12, HALO, D)
     copies = send_cells(lat, lon, border_grad, cells_back, True, back_send, back_recv)
-    received = dot(onehot_rows(receivers, 0, NODE), dpre[...]).astype(BF)
+    received = dot(to_receiver[...], hats[...]).astype(BF)
     picked = onehot_rows([group_row(groups)], 0, NODE)
-    center = jnp.concatenate([border_grad[cell] for cell in (5, 6, 9, 10)], axis=0)
-    total[...] += table_grad(0) + dot_t(received, wr[...]) + dot(picked, center)
+    rows = dot(onehot_rows(senders, 0, OUTER), hats[...])
+    rows = rows[0:NODE] + dot(picked, rows[NODE:OUTER].astype(BF))
+    total[...] += dot_t(rows.astype(BF), ws[...]) + dot_t(received, wr[...])
+
+    def grads(i, carry):
+        at = pl.ds(pl.multiple_of(i * TILE, TILE), TILE)
+        pre[at, :] = cot[at, :].astype(F32) + dot_t(hats[at, :], we[...])
+        pltpu.make_async_copy(pre.at[at, :], grad_h.at[at, :], grad_sems.at[i]).start()
+        return carry
+
+    lax.fori_loop(0, EDGE // TILE, grads, 0)
     for copy in copies:
         copy.wait()
     summed = dot(picked, cells_back[0:4].reshape(128, D))
@@ -341,44 +414,25 @@
     total_copy.start()
     for i in range(EDGE // TILE):
         at = pl.ds(i * TILE, TILE)
-        pltpu.make_async_copy(edge_out.at[at, :], edge_out_h.at[at, :], edge_sems.at[i]).wait()
-        pltpu.make_async_copy(dpre.at[at, :], dpre_h.at[at, :], dpre_sems.at[i]).wait()
+        pltpu.make_async_copy(edge.at[at, :], edge_out_h.at[at, :], edge_sems.at[i]).wait()
+        pltpu.make_async_copy(pre.at[at, :], grad_h.at[at, :], grad_sems.at[i]).wait()
     node_copy.wait()
     total_copy.wait()
 
 
-def finish_kernel(
-    edge_i, node_i, total_i, dpre_h, cot_h, we_h, edge_o, node_o, total_o, grad_o,
-    dpre, cot, we, grad, pass_sems, we_sem, dpre_sems, cot_sems, grad_sems,
-):
-    weight = pltpu.make_async_copy(we_h, we, we_sem)
-    weight.start()
-    tiles = [pl.ds(i * TILE, TILE) for i in range(EDGE // TILE)]
-    loads = []
-    for i, at in enumerate(tiles):
-        pair = (
-            pltpu.make_async_copy(dpre_h.at[at, :], dpre.at[at, :], dpre_sems.at[i]),
-            pltpu.make_async_copy(cot_h.at[at, :], cot.at[at, :], cot_sems.at[i]),
-        )
-        for copy in pair:
-            copy.start()
-        loads.append(pair)
-    passed = [
-        pltpu.make_async_copy(src, dst, pass_sems.at[i])
-        for i, (src, dst) in enumerate(((edge_i, edge_o), (node_i, node_o), (total_i, total_o)))
-    ]
-    for copy in passed:
+def finish_kernel(edge_i, grad_i, node_i, total_i, edge_o, grad_o, node_o, total_o, sems):
+    copies = []
+    for i in range(8):
+        at = pl.ds(i * (EDGE // 8), EDGE // 8)
+        copies.append((grad_i.at[at, :], grad_o.at[at, :]))
+    for i in range(4):
+        at = pl.ds(i * (EDGE // 4), EDGE // 4)
+        copies.append((edge_i.at[at, :], edge_o.at[at, :]))
+    copies += [(total_i, total_o), (node_i, node_o)]
+    copies = [pltpu.make_async_copy(*pair, sems.at[i]) for i, pair in enumerate(copies)]
+    for copy in copies:
         copy.start()
-    weight.wait()
-    stores = []
-    for i, at in enumerate(tiles):
-        for copy in loads[i]:
-            copy.wait()
-        grad[at, :] = cot[at, :].astype(F32) + dot_t(dpre[at, :], we[...])
-        store = pltpu.make_async_copy(grad.at[at, :], grad_o.at[at, :], grad_sems.at[i])
-        store.start()
-        stores.append(store)
-    for copy in passed + stores:
+    for copy in copies:
         copy.wait()
 
 
@@ -408,18 +462,19 @@
     any_space = pl.BlockSpec(memory_space=pl.ANY)
     hbm = pl.BlockSpec(memory_space=pltpu.HBM)
     line = pltpu.VMEM((1, D), F32)
+    outer = pltpu.VMEM((12, HALO, D), BF)
     slot_rows = pltpu.VMEM((EDGE // 128, 128), jnp.int32)
     keep = lambda v: pltpu.with_memory_space_constraint(v, pltpu.HBM)
     vector = lambda v: v.reshape(1, D)
     results = (
         jax.ShapeDtypeStruct((EDGE, D), BF),
+        jax.ShapeDtypeStruct((EDGE, D), F32),
         jax.ShapeDtypeStruct((NODE, D), BF),
         jax.ShapeDtypeStruct((NODE, D), F32),
     )
-    edges = jax.ShapeDtypeStruct((EDGE, D), BF)
-    edge_result, dpre, node_result, node_grad = pl.pallas_call(
+    done = pl.pallas_call(
         layer_kernel,
-        out_shape=(results[0], edges, results[1], results[2]),
+        out_shape=results,
         in_specs=[pl.BlockSpec(memory_space=pltpu.SMEM)] + [hbm] * 21,
         out_specs=(any_space,) * 4,
         scratch_shapes=[
@@ -430,9 +485,11 @@
         + [
             cells, wide, chunk, chunk, pltpu.VMEM((NODE + BORDER + FAR, D), BF), nodes,
             column_of, column_of, full,
-            half, half, half, half, half, pltpu.VMEM((EDGE, 1), F32), nodes, nodes,
+            half, half, pltpu.VMEM((EDGE, 1), F32), nodes, nodes,
             pltpu.VMEM((NODE, D), F32),
-            cells, chunk, chunk, pltpu.VMEM((12, HALO, D), BF),
+            outer, chunk, chunk, outer,
+            pltpu.VMEM((EDGE, NODE), BF), pltpu.VMEM((EDGE, REMOTE), BF),
+            pltpu.VMEM((NODE, EDGE), BF), pltpu.VMEM((FAR, EDGE), BF),
             sems((21,)), tiles, tiles, sems((2,)), sems((6,)),
             sems((12,)), sems((12,)), sems((12,)), sems((12,)),
         ],
@@ -450,15 +507,15 @@
         node_cotangent, edge_cotangent,
         )),
     )
-    edge_result, node_result, node_grad, edge_grad = pl.pallas_call(
+    edge_result, edge_grad, node_result, node_grad = pl.pallas_call(
         finish_kernel,
-        out_shape=(*results, jax.ShapeDtypeStruct((EDGE, D), F32)),
-        in_specs=[any_space] * 4 + [hbm] * 2,
+        out_shape=results,
+        in_specs=[any_space] * 4,
         out_specs=(any_space,) * 4,
-        scratch_shapes=[half, half, weight, full, sems((3,)), sems, tiles, tiles, tiles],
-        compiler_params=pltpu.CompilerParams(vmem_limit_bytes=16 * 1024 * 1024),
+        scratch_shapes=[sems((14,))],
+        compiler_params=pltpu.CompilerParams(vmem_limit_bytes=1024 * 1024),
         name="finish",
-    )(edge_result, node_result, node_grad, dpre, keep(edge_cotangent), keep(edge_weight))
+    )(*done)
     return node_result, edge_result, node_grad, edge_grad
 
 

time: 59.2 us -> 53.5 us (0.904)
  Pallas kernels: 57.7 us -> 51.9 us
    pallas_call x2, Pallas kernels: 57.7 us -> 51.9 us  [the longest x1 48.9 us: per_device(): pl.pallas_call(layer_kernel, out_shape=results, in_specs=[pl.BlockSpec(me...]
where the time goes in v3:
time: 53.5 us; the launch traced here: 53.4 us
  Pallas kernels  51.9 us (97%)
  between operations  1.45 us (3%)
    pallas_call x1, Pallas kernels, per_device(): pl.pallas_call(layer_kernel, out_shape=results, in_specs=[pl.BlockSpec(me...  48.9 us
    pallas_call x1, Pallas kernels, per_device(): pl.pallas_call(finish_kernel, out_shape=results, in_specs=[any_space] * 4...  3 us

profile of v3, /device:TPU:1, one launch (start us, length us, event | category | flops | bytes accessed | tf_op | source)
XLA Modules:
  0.0 53.4 jit_solution(8142954827375749959)
XLA Ops:
  1.3 48.9 %layer.1 = (bf16[2048,512]{1,0:T(8,128)(2,1)S(1)}, f32[2048,512]{1,0:T(8,128)S(1)}, bf16[256,512]{1,0:T(8,128)(2,1)S(1)}, f32[256,512]{1,0:T(8,128)S(1)}) custom-call(s32[1]{0:T(128)S(6)} %copy.26.count, bf16[256,512]{1,0:T(8,128)(2,1)} %node_h.1, s32[1,2,2,32]{3,2,1,0:T(2,128)} %groups_h.1, s32[1,4,128]{2,1,0:T(4,128)} %bitcast.11, bf16[512,512]{1,0:T(8,128)(2,1)} %ws_h.1, ...), custom_call_target="tpu_custom_call" | custom-call | tf_op jit(solution)/shard_map/layer/pallas_call | solution.py:475
  50.2 3.0 %finish.1 = (bf16[2048,512]{1,0:T(8,128)(2,1)}, f32[2048,512]{1,0:T(8,128)}, bf16[256,512]{1,0:T(8,128)(2,1)}, f32[256,512]{1,0:T(8,128)}) custom-call(bf16[2048,512]{1,0:T(8,128)(2,1)S(1)} %get-tuple-element.12.edge_i, f32[2048,512]{1,0:T(8,128)S(1)} %get-tuple-element.13.grad_i, bf16[256,512]{1,0:T(8,128)(2,1)S(1)} %get-tuple-element.14.node_i, ...), custom_call_target="tpu_custom_call" | custom-call | tf_op jit(solution)/shard_map/finish/pallas_call | solution.py:510

commit v4 on v3

--- a/solution.py
+++ b/solution.py
@@ -94,7 +94,8 @@
     me = lat * N_LON + lon
 
     def one(step, carry):
-        peer = lax.rem(me + step, DEVICES)
+        apart = DEVICES // 2 + (step // 2) * (1 - 2 * lax.rem(step, 2))
+        peer = lax.rem(me + apart, DEVICES)
         pltpu.make_async_remote_copy(
             src_ref=source.at[peer],
             dst_ref=target.at[me],

time: 53.5 us -> 53.6 us (level)
  no operation moved by 1% of the time
where the time goes in v4:
time: 53.6 us; the launch traced here: 53.5 us
  Pallas kernels  52.1 us (97%)
  between operations  1.45 us (3%)
    pallas_call x1, Pallas kernels, per_device(): pl.pallas_call(layer_kernel, out_shape=results, in_specs=[pl.BlockSpec(me...  49.1 us
    pallas_call x1, Pallas kernels, per_device(): pl.pallas_call(finish_kernel, out_shape=results, in_specs=[any_space] * 4...  3 us

profile of v4, /device:TPU:1, one launch (start us, length us, event | category | flops | bytes accessed | tf_op | source)
XLA Modules:
  0.0 53.5 jit_solution(17210776079577039888)
XLA Ops:
  1.3 49.1 %layer.1 = (bf16[2048,512]{1,0:T(8,128)(2,1)S(1)}, f32[2048,512]{1,0:T(8,128)S(1)}, bf16[256,512]{1,0:T(8,128)(2,1)S(1)}, f32[256,512]{1,0:T(8,128)S(1)}) custom-call(s32[1]{0:T(128)S(6)} %copy.26.count, bf16[256,512]{1,0:T(8,128)(2,1)} %node_h.1, s32[1,2,2,32]{3,2,1,0:T(2,128)} %groups_h.1, s32[1,4,128]{2,1,0:T(4,128)} %bitcast.11, bf16[512,512]{1,0:T(8,128)(2,1)} %ws_h.1, ...), custom_call_target="tpu_custom_call" | custom-call | tf_op jit(solution)/shard_map/layer/pallas_call | solution.py:476
  50.4 3.0 %finish.1 = (bf16[2048,512]{1,0:T(8,128)(2,1)}, f32[2048,512]{1,0:T(8,128)}, bf16[256,512]{1,0:T(8,128)(2,1)}, f32[256,512]{1,0:T(8,128)}) custom-call(bf16[2048,512]{1,0:T(8,128)(2,1)S(1)} %get-tuple-element.12.edge_i, f32[2048,512]{1,0:T(8,128)S(1)} %get-tuple-element.13.grad_i, bf16[256,512]{1,0:T(8,128)(2,1)S(1)} %get-tuple-element.14.node_i, ...), custom_call_target="tpu_custom_call" | custom-call | tf_op jit(solution)/shard_map/finish/pallas_call | solution.py:511
